TPU v7x, 32 devices: a whole 2x2x4 slice. The times are simulated.
32 devices in a mesh: mode: 4 (over z), slab: 8 (over y, x, core).
Axes of the slice: x: 2, y: 2, z: 4, core: 2. Of those that a mesh axis runs over, the one named last changes fastest.
Arguments:
- modes: bfloat16 [48, 3, 16, 64, 128], P('mode', None, 'slab'), may hold values from -100 to 100
- volume: float32 [16, 64, 128], P(None, ('mode', 'slab')), may hold values from 0.5 to 24
Outputs:
- convective: float32 [2304, 48], P(('mode', 'slab'))
- dissipation: float32 [48, 48], replicated
All inputs are finite; a program needn't handle non-finite values.
Results may differ from a plain program's by a relative error of at most 0.0043.
Values may be sent and summed in bfloat16 or wider, within the bound.
No kernel may reach another device: no remote copies, remote signals or barrier semaphores. Data moves between devices by JAX's collectives and lax.ppermute only.
A program may use at most 128 MiB of HBM per device.

v0:
```python
import math

import jax
import jax.numpy as jnp
from jax import lax
from jax.sharding import PartitionSpec as P

viscosity = 0.05


def extended(block, sides, width):
    for axis, dim in sides:
        count = lax.axis_size(axis)
        forward = [(i, i + 1) for i in range(count - 1)]
        backward = [(target, source) for source, target in forward]
        low = lax.ppermute(
            lax.slice_in_dim(block, block.shape[dim] - width, None, axis=dim), axis, forward
        )
        high = lax.ppermute(lax.slice_in_dim(block, 0, width, axis=dim), axis, backward)
        block = jnp.concatenate([low, block, high], axis=dim)
    return block


def stencil(padded, dim, length):
    shifted = [
        lax.slice_in_dim(padded, offset, offset + length, axis=dim).astype(jnp.float32)
        for offset in range(5)
    ]
    return (shifted[0] - 8.0 * shifted[1] + 8.0 * shifted[3] - shifted[4]) / 12.0


def gradient_fields(centre, x_padded, y_padded):
    z_padded = jnp.concatenate([centre[..., -2:], centre, centre[..., :2]], axis=4)
    along_x = stencil(x_padded, 2, centre.shape[2])
    along_y = stencil(y_padded, 3, centre.shape[3])
    along_z = stencil(z_padded, 4, centre.shape[4])
    return jnp.stack([along_x, along_y, along_z], axis=2).astype(jnp.bfloat16)


def regroup(stacked):
    return lax.all_to_all(
        lax.all_to_all(stacked, "mode", split_axis=3, concat_axis=0, tiled=True),
        "slab",
        split_axis=3,
        concat_axis=2,
        tiled=True,
    )


def contract(values, grad_all, weights, limit):
    mode_count = values.shape[0]
    cell_count = weights.size
    block_size = math.gcd(cell_count, limit)
    flat_values = values.reshape(mode_count, 3, cell_count)
    flat_grads = grad_all.reshape(mode_count, 3, 3, cell_count)
    flat_weights = weights.reshape(cell_count)

    def one_step(number, running):
        first_cell = number * block_size
        piece_values = lax.dynamic_slice_in_dim(flat_values, first_cell, block_size, 2)
        piece_grads = lax.dynamic_slice_in_dim(flat_grads, first_cell, block_size, 3)
        piece_weights = lax.dynamic_slice_in_dim(flat_weights, first_cell, block_size, 0)
        values_wide = piece_values.astype(jnp.float32)
        grads_wide = piece_grads.astype(jnp.float32)
        carried = values_wide[:, None, None, 0, :] * grads_wide[None, :, :, 0, :]
        carried = carried + values_wide[:, None, None, 1, :] * grads_wide[None, :, :, 1, :]
        carried = carried + values_wide[:, None, None, 2, :] * grads_wide[None, :, :, 2, :]
        carried = (
            (carried * piece_weights)
            .astype(jnp.bfloat16)
            .reshape(mode_count * mode_count, 3 * block_size)
        )
        conv_add = lax.dot_general(
            piece_values.reshape(mode_count, 3 * block_size),
            carried,
            (((1,), (1,)), ((), ())),
            preferred_element_type=jnp.float32,
        )
        weighted = (
            (grads_wide * piece_weights).astype(jnp.bfloat16).reshape(mode_count, 9 * block_size)
        )
        diss_add = lax.dot_general(
            piece_grads.reshape(mode_count, 9 * block_size),
            weighted,
            (((1,), (1,)), ((), ())),
            preferred_element_type=jnp.float32,
        )
        return (running[0] + conv_add, running[1] + diss_add)

    start_conv = jnp.zeros((mode_count, mode_count * mode_count), jnp.float32)
    start_diss = jnp.zeros((mode_count, mode_count), jnp.float32)
    conv_sum, diss_sum = lax.fori_loop(
        0, cell_count // block_size, one_step, (start_conv, start_diss)
    )
    return (conv_sum.reshape(mode_count * mode_count, mode_count), diss_sum)


def per_device(modes, volume):
    x_padded = extended(modes, (("slab", 2),), 2)
    y_padded = jnp.pad(modes, ((0, 0), (0, 0), (0, 0), (2, 2), (0, 0)))
    local_grads = gradient_fields(modes, x_padded, y_padded)
    local_count = modes.shape[0]
    stacked = jnp.concatenate(
        [modes, local_grads.reshape((local_count, 9) + modes.shape[2:])], axis=1
    )
    regrouped = regroup(stacked)
    values = regrouped[:, :3]
    grad_all = regrouped[:, 3:].reshape((regrouped.shape[0], 3, 3) + regrouped.shape[2:])
    conv_part, diss_part = contract(values, grad_all, volume, 1024)
    conv_sum = lax.psum_scatter(conv_part, ("mode", "slab"), scatter_dimension=0, tiled=True)
    diss_sum = lax.psum(diss_part, ("mode", "slab"))
    cell_total = (
        volume.shape[0]
        * volume.shape[1]
        * volume.shape[2]
        * lax.axis_size("mode")
        * lax.axis_size("slab")
    )
    convective = conv_sum * (1.0 / math.sqrt(cell_total))
    dissipation = diss_sum * (viscosity / cell_total)
    return (convective, dissipation)


def solution(mesh):
    placed = (P("mode", None, "slab", None, None), P(None, ("mode", "slab"), None))
    return jax.shard_map(
        per_device,
        mesh=mesh,
        in_specs=placed,
        out_specs=(P(("mode", "slab"), None), P()),
        check_vma=False,
    )
```

profile of v0, /device:TPU:0, one launch (start us, length us, event | category | flops | bytes accessed | tf_op | source)
XLA Modules:
  0.0 560.6 jit_solution(18260049070888457423)
XLA Ops:
  7.2 1.4 collective-permute-start.1
  8.6 3.1 collective-permute-start
  11.7 2.2 fusion.10
  14.3 5.0 fusion.4
  19.8 2.5 pad_maximum_fusion
  22.3 9.4 %copy.58 = bf16[12,12,2,64,128]{4,2,1,0,3:T(2,128)(2,1)} copy(bf16[12,12,2,64,128]{4,3,2,1,0:T(8,128)(2,1)} %pad_maximum_fusion) | data formatting | bytes 9437184 | tf_op jit(solution)/shard_map/concatenate | solution.py:103
  31.7 105.4 %all_to_all.36 = bf16[12,12,2,64,128]{4,2,1,0,3:T(2,128)(2,1)S(1)} all-to-all(bf16[12,12,2,64,128]{4,2,1,0,3:T(2,128)(2,1)} %copy.58), channel_id=1, replica_groups=mesh['mode'=4,'slab'=8] {'mode'}, dimensions={3} | all-to-all | bytes 9437184 | tf_op jit(solution)/shard_map/all_to_all | solution.py:42
  137.1 3.0 copy.59
  140.1 3.5 copy.60
  143.7 9.0 %copy.61 = bf16[48,12,2,16,128]{4,2,1,0,3:T(2,128)(2,1)} copy(bf16[48,12,2,16,128]{4,3,2,1,0:T(8,128)(2,1)} %bitcast.76) | data formatting | bytes 9437184 | tf_op jit(solution)/shard_map/all_to_all | solution.py:42
  152.7 31.1 %all-to-all-start.1 = ((bf16[48,12,2,16,128]{4,2,1,0,3:T(2,128)(2,1)}), bf16[48,12,2,16,128]{4,2,1,0,3:T(2,128)(2,1)}, u32[]{:S(2)}, u32[]{:S(2)}) async-start(bf16[48,12,2,16,128]{4,2,1,0,3:T(2,128)(2,1)} %copy.61), calls=%async_computation.1 | async-start | bytes 9437184 | tf_op jit(solution)/shard_map/all_to_all | solution.py:41
  183.8 54.8 %all-to-all-done.1 = bf16[48,12,2,16,128]{4,2,1,0,3:T(2,128)(2,1)} async-done(((bf16[48,12,2,16,128]{4,2,1,0,3:T(2,128)(2,1)}), bf16[48,12,2,16,128]{4,2,1,0,3:T(2,128)(2,1)}, u32[]{:S(2)}, u32[]{:S(2)}) %all-to-all-start.1) | async-done | bytes 4718624 | tf_op jit(solution)/shard_map/all_to_all | solution.py:41
  238.6 3.4 copy.62
  242.0 1.5 copy.63
  243.4 1.1 slice.120
  245.1 3.0 copy.65
  248.1 4.4 reshape_reshape.3
  252.5 2.2 copy.69
  255.1 200.4 %while.16 = (s32[]{:T(128)}, f32[48,2304]{1,0:T(8,128)}, f32[48,48]{1,0:T(8,128)S(1)}, bf16[48,3,4096]{2,1,0:T(4,128)(2,1)S(1)}, bf16[48,3,3,4096]{3,0,2,1:T(8,1...) while((s32[]{:T(128)}, f32[48,2304]{1,0:T(8,128)}, ...), condition=%wide.region_1.2_spmd.clone, body=%wide.region_0.1_spmd.clone.sunk | while | flops 773485056 | bytes 84676336 | solution.py:92
  255.2 0.7 dynamic_slice.40
  255.9 1.9 fusion.22
  258.5 0.8 copy_bitcast_fusion.4
  259.4 1.4 dynamic-slice_convert_fusion.3
  261.0 1.3 copy.89
  262.3 1.3 copy.90
  263.6 1.3 copy.91
  264.9 19.9 %multiply_convert_fusion.9 = bf16[48,48,3,1024]{3,2,1,0:T(4,128)(2,1)S(1)} fusion(f32[1024]{0:T(1024)S(1)} %dynamic_slice.40, f32[48,3,1024]{2,1,0:T(4,128)} %copy.89, f32[48,1024]{1,0:T(8,128)} %get-tuple-element.248, f32[48,3,1024]{2,1,0:T(4,128)} %copy.90, f32[48,1024]{1,0:T(8,128)} %get-tuple-element.250, f32[48,3,1024]{2,1,0:T(4,128)} %copy.91, ...), kind=kLoop, calls=%fused_computation.clone.1 | loop fusion | flops 49545216 | bytes 16519168 | tf_op jit(solution)/shard_map/while/body/eval_jaxpr/convert_element_type | solution.py:70
  284.8 10.3 %copy.93 = bf16[288,8,3,1024]{3,1,2,0:T(8,128)(2,1)} copy(bf16[288,8,3,1024]{3,2,1,0:T(4,128)(2,1)S(1)} %bitcast.68) | data formatting | bytes 28311552 | tf_op jit(solution)/shard_map/while
  295.0 10.2 %convolution_add_fusion.2 = f32[48,2304]{1,0:T(8,128)} fusion(bf16[48,3072]{1,0:T(8,128)(2,1)S(1)} %bitcast.71, bf16[2304,3072]{1,0:T(8,128)(2,1)} %bitcast.69, f32[48,2304]{1,0:T(8,128)} %get-tuple-element.264, pred[]{:T(512)S(6)} %compare.4), kind=kOutput, calls=%fused_computation.1.clone.1 | convolution fusion | flops 679698432 | bytes 15335425 | tf_op jit(solution)/shard_map/while/body/eval_jaxpr/dot_general | solution.py:73
  305.3 0.7 dynamic_slice.40
  306.0 1.9 fusion.22
  308.6 0.8 copy_bitcast_fusion.4
  309.4 1.4 dynamic-slice_convert_fusion.3
  311.0 1.3 copy.89
  312.3 1.3 copy.90
  313.6 1.3 copy.91
  314.9 19.9 %multiply_convert_fusion.9 = bf16[48,48,3,1024]{3,2,1,0:T(4,128)(2,1)S(1)} fusion(f32[1024]{0:T(1024)S(1)} %dynamic_slice.40, f32[48,3,1024]{2,1,0:T(4,128)} %copy.89, f32[48,1024]{1,0:T(8,128)} %get-tuple-element.248, f32[48,3,1024]{2,1,0:T(4,128)} %copy.90, f32[48,1024]{1,0:T(8,128)} %get-tuple-element.250, f32[48,3,1024]{2,1,0:T(4,128)} %copy.91, ...), kind=kLoop, calls=%fused_computation.clone.1 | loop fusion | flops 49545216 | bytes 16519168 | tf_op jit(solution)/shard_map/while/body/eval_jaxpr/convert_element_type | solution.py:70
  334.8 10.3 %copy.93 = bf16[288,8,3,1024]{3,1,2,0:T(8,128)(2,1)} copy(bf16[288,8,3,1024]{3,2,1,0:T(4,128)(2,1)S(1)} %bitcast.68) | data formatting | bytes 28311552 | tf_op jit(solution)/shard_map/while
  345.1 10.3 %convolution_add_fusion.2 = f32[48,2304]{1,0:T(8,128)} fusion(bf16[48,3072]{1,0:T(8,128)(2,1)S(1)} %bitcast.71, bf16[2304,3072]{1,0:T(8,128)(2,1)} %bitcast.69, f32[48,2304]{1,0:T(8,128)} %get-tuple-element.264, pred[]{:T(512)S(6)} %compare.4), kind=kOutput, calls=%fused_computation.1.clone.1 | convolution fusion | flops 679698432 | bytes 15335425 | tf_op jit(solution)/shard_map/while/body/eval_jaxpr/dot_general | solution.py:73
  355.3 0.7 dynamic_slice.40
  356.0 1.9 fusion.22
  358.6 0.8 copy_bitcast_fusion.4
  359.5 1.4 dynamic-slice_convert_fusion.3
  361.0 1.3 copy.89
  362.4 1.3 copy.90
  363.7 1.3 copy.91
  364.9 19.9 %multiply_convert_fusion.9 = bf16[48,48,3,1024]{3,2,1,0:T(4,128)(2,1)S(1)} fusion(f32[1024]{0:T(1024)S(1)} %dynamic_slice.40, f32[48,3,1024]{2,1,0:T(4,128)} %copy.89, f32[48,1024]{1,0:T(8,128)} %get-tuple-element.248, f32[48,3,1024]{2,1,0:T(4,128)} %copy.90, f32[48,1024]{1,0:T(8,128)} %get-tuple-element.250, f32[48,3,1024]{2,1,0:T(4,128)} %copy.91, ...), kind=kLoop, calls=%fused_computation.clone.1 | loop fusion | flops 49545216 | bytes 16519168 | tf_op jit(solution)/shard_map/while/body/eval_jaxpr/convert_element_type | solution.py:70
  384.8 10.3 %copy.93 = bf16[288,8,3,1024]{3,1,2,0:T(8,128)(2,1)} copy(bf16[288,8,3,1024]{3,2,1,0:T(4,128)(2,1)S(1)} %bitcast.68) | data formatting | bytes 28311552 | tf_op jit(solution)/shard_map/while
  395.1 10.3 %convolution_add_fusion.2 = f32[48,2304]{1,0:T(8,128)} fusion(bf16[48,3072]{1,0:T(8,128)(2,1)S(1)} %bitcast.71, bf16[2304,3072]{1,0:T(8,128)(2,1)} %bitcast.69, f32[48,2304]{1,0:T(8,128)} %get-tuple-element.264, pred[]{:T(512)S(6)} %compare.4), kind=kOutput, calls=%fused_computation.1.clone.1 | convolution fusion | flops 679698432 | bytes 15335425 | tf_op jit(solution)/shard_map/while/body/eval_jaxpr/dot_general | solution.py:73
  405.4 0.7 dynamic_slice.40
  406.1 2.0 fusion.22
  408.8 0.8 copy_bitcast_fusion.4
  409.7 1.4 dynamic-slice_convert_fusion.3
  411.2 1.3 copy.89
  412.5 1.3 copy.90
  413.9 1.3 copy.91
  415.1 19.9 %multiply_convert_fusion.9 = bf16[48,48,3,1024]{3,2,1,0:T(4,128)(2,1)S(1)} fusion(f32[1024]{0:T(1024)S(1)} %dynamic_slice.40, f32[48,3,1024]{2,1,0:T(4,128)} %copy.89, f32[48,1024]{1,0:T(8,128)} %get-tuple-element.248, f32[48,3,1024]{2,1,0:T(4,128)} %copy.90, f32[48,1024]{1,0:T(8,128)} %get-tuple-element.250, f32[48,3,1024]{2,1,0:T(4,128)} %copy.91, ...), kind=kLoop, calls=%fused_computation.clone.1 | loop fusion | flops 49545216 | bytes 16519168 | tf_op jit(solution)/shard_map/while/body/eval_jaxpr/convert_element_type | solution.py:70
  435.0 10.3 %copy.93 = bf16[288,8,3,1024]{3,1,2,0:T(8,128)(2,1)} copy(bf16[288,8,3,1024]{3,2,1,0:T(4,128)(2,1)S(1)} %bitcast.68) | data formatting | bytes 28311552 | tf_op jit(solution)/shard_map/while
  445.3 10.3 %convolution_add_fusion.2 = f32[48,2304]{1,0:T(8,128)} fusion(bf16[48,3072]{1,0:T(8,128)(2,1)S(1)} %bitcast.71, bf16[2304,3072]{1,0:T(8,128)(2,1)} %bitcast.69, f32[48,2304]{1,0:T(8,128)} %get-tuple-element.264, pred[]{:T(512)S(6)} %compare.4), kind=kOutput, calls=%fused_computation.1.clone.1 | convolution fusion | flops 679698432 | bytes 15335425 | tf_op jit(solution)/shard_map/while/body/eval_jaxpr/dot_general | solution.py:73
  455.6 2.8 reshape.95
  458.3 38.1 %psum.7 = f32[48,48]{1,0:T(8,128)S(1)} all-reduce(f32[48,48]{1,0:T(8,128)S(1)} %get-tuple-element.113), channel_id=1, replica_groups=mesh['mode'=4,'slab'=8] {'mode','slab'}, use_global_device_ids=true, to_apply=%region_3.4 | all-reduce | flops 2304 | bytes 18432 | tf_op jit(solution)/shard_map/psum | solution.py:111
  497.1 55.2 %reduce-scatter.4.cloned.1.call-done = f32[72,48]{1,0:T(8,128)} async-done(((f32[2304,48]{1,0:T(8,128)}), f32[72,48]{1,0:T(8,128)}) %reduce-scatter.4.cloned.1.call-update) | async-done | bytes 13840
  552.3 0.8 broadcast_multiply_fusion
  553.1 0.7 copy.67
  (50 shorter events, 6.2 us)
Async XLA Ops:
  7.2 7.1 %copy-start = (bf16[12,3,2,64,128]{4,3,2,1,0:T(8,128)(2,1)S(1)}, bf16[12,3,2,64,128]{4,3,2,1,0:T(8,128)(2,1)}, u32[]{:S(2)}) copy-start(bf16[12,3,2,64,128]{4,3,2,1,0:T(8,128)(2,1)} %param.4) | copy-start | bytes 3538948
  7.2 6.8 %collective-permute-start.1 = (bf16[12,3,2,64,128]{4,3,2,1,0:T(8,128)(2,1)}, bf16[12,3,2,64,128]{4,3,2,1,0:T(8,128)(2,1)S(1)}, u32[]{:S(2)}, u32[]{:S(2)}) collective-permute-start(bf16[12,3,2,64,128]{4,3,2,1,0:T(8,128)(2,1)} %param.4), channel_id=1, source_target_pairs={{1,0},{2,1},{3,2},{4,3},{5,4},{6,5},{7,6},{9,8},{10,9},{11,10},{12... | collective-permute-start | bytes 3538952 | tf_op jit(solution)/shard_map/ppermute | solution.py:19
  8.6 5.7 %collective-permute-start = (bf16[12,3,2,64,128]{4,3,2,1,0:T(8,128)(2,1)}, bf16[12,3,2,64,128]{4,3,2,1,0:T(8,128)(2,1)S(1)}, u32[]{:S(2)}, u32[]{:S(2)}) collective-permute-start(bf16[12,3,2,64,128]{4,3,2,1,0:T(8,128)(2,1)} %param.4), channel_id=1, source_target_pairs={{0,1},{1,2},{2,3},{3,4},{4,5},{5,6},{6,7},{8,9},{9,10},{10,11},{11... | collective-permute-start | bytes 3538952 | tf_op jit(solution)/shard_map/ppermute | solution.py:16
  152.7 85.9 %all-to-all-start.1 = ((bf16[48,12,2,16,128]{4,2,1,0,3:T(2,128)(2,1)}), bf16[48,12,2,16,128]{4,2,1,0,3:T(2,128)(2,1)}, u32[]{:S(2)}, u32[]{:S(2)}) async-start(bf16[48,12,2,16,128]{4,2,1,0,3:T(2,128)(2,1)} %copy.61), calls=%async_computation.1 | async-start | bytes 9437184 | tf_op jit(solution)/shard_map/all_to_all | solution.py:41
  183.8 368.5 %reduce-scatter.4.cloned.1.call-start = ((), (), s32[]{:S(2)}) async-start(), calls=%async_computation.3 | async-start | bytes 1216512
  252.5 2.6 copy-start.3
  255.2 4.2 copy-start.1
  295.0 10.2 %copy-start.2 = (bf16[48,3,4096]{2,1,0:T(4,128)(2,1)S(1)}, bf16[48,3,4096]{2,1,0:T(4,128)(2,1)}, u32[]{:S(2)}) copy-start(bf16[48,3,4096]{2,1,0:T(4,128)(2,1)} %copy-done.1) | copy-start | bytes 3538948 | tf_op jit(solution)/shard_map/while
  305.3 4.1 copy-start.1
  345.1 10.3 %copy-start.2 = (bf16[48,3,4096]{2,1,0:T(4,128)(2,1)S(1)}, bf16[48,3,4096]{2,1,0:T(4,128)(2,1)}, u32[]{:S(2)}) copy-start(bf16[48,3,4096]{2,1,0:T(4,128)(2,1)} %copy-done.1) | copy-start | bytes 3538948 | tf_op jit(solution)/shard_map/while
  355.3 4.1 copy-start.1
  395.1 10.3 %copy-start.2 = (bf16[48,3,4096]{2,1,0:T(4,128)(2,1)S(1)}, bf16[48,3,4096]{2,1,0:T(4,128)(2,1)}, u32[]{:S(2)}) copy-start(bf16[48,3,4096]{2,1,0:T(4,128)(2,1)} %copy-done.1) | copy-start | bytes 3538948 | tf_op jit(solution)/shard_map/while
  405.4 4.2 copy-start.1
  445.3 10.3 %copy-start.2 = (bf16[48,3,4096]{2,1,0:T(4,128)(2,1)S(1)}, bf16[48,3,4096]{2,1,0:T(4,128)(2,1)}, u32[]{:S(2)}) copy-start(bf16[48,3,4096]{2,1,0:T(4,128)(2,1)} %copy-done.1) | copy-start | bytes 3538948 | tf_op jit(solution)/shard_map/while
Sparse Core Ops, SparseCore 0:
  458.5 93.7 reduce-scatter.3
where the time goes:
time: 562 us; the launch traced here: 561 us
  blocking collectives  144 us (26%)
  local copies, waits for them, and re-layouts  114 us (20%)
  waiting for transfers between devices  110 us (20%)
  other arithmetic  94.4 us (17%)
  matrix products  48.7 us (9%)
  starting transfers between devices  35.6 us (6%)
  between operations  14.2 us (3%)
    all_to_all x1, blocking collectives, regroup(): lax.all_to_all(stacked, 'mode', split_axis=3, concat_axis=0, tiled=True)  105 us
    convert_element_type x4, other arithmetic, one_step(): carried = (carried * piece_weights).astype(jnp.bfloat16).reshape(mode_cou...  79.5 us
    unnamed x2, waiting for transfers between devices  55.2 us
    all_to_all x1, waiting for transfers between devices, regroup(): lax.all_to_all(lax.all_to_all(stacked, 'mode', split_axis=3, concat_axis=...  54.8 us
    while x32, local copies, waits for them, and re-layouts  45 us
    dot_general x4, matrix products, one_step(): lax.dot_general(piece_values.reshape(mode_count, 3 * block_size), carried...  41 us
    psum x1, blocking collectives, per_device(): diss_sum = lax.psum(diss_part, ('mode', 'slab'))  38.1 us
    all_to_all x1, starting transfers between devices, regroup(): lax.all_to_all(lax.all_to_all(stacked, 'mode', split_axis=3, concat_axis=...  31.1 us
  transfers between devices with their start and end apart: 4, of which 3 were waited for; matrix products, arithmetic and copies ran while one was open for 1% of the time, Pallas kernels for 0%

commit v1 on v0

v1 whole, which is shorter than its diff:
```python
import functools
import math

import jax
import jax.numpy as jnp
from jax import lax
from jax.experimental import pallas as pl
from jax.experimental.pallas import tpu as pltpu
from jax.sharding import PartitionSpec as P

viscosity = 0.05
bf16 = jnp.bfloat16
f32 = jnp.float32
VMEM_LIMIT = 56 * 2**20
FIRST = 0.5

vmem = pl.BlockSpec(memory_space=pltpu.VMEM)
smem = pl.BlockSpec(memory_space=pltpu.SMEM)


def assemble_kernel(me_ref, *refs):
    blocks, out_ref, wide = refs[:-2], refs[-2], refs[-1]
    local = blocks[0].shape[1] // 6
    total = local * len(blocks)

    def one_row(row, unused):
        for shift, block in enumerate(blocks):
            owner = me_ref[0] ^ shift
            values = block[row].astype(f32)
            for part in range(6):
                for piece in range(wide.shape[0]):
                    wide[piece, pl.ds(part * total + owner * local, local), :] = values[
                        part * local : (part + 1) * local, piece * 128 : (piece + 1) * 128
                    ]
        for piece in range(wide.shape[0]):
            out_ref[row, :, piece * 128 : (piece + 1) * 128] = wide[piece].astype(bf16)
        return unused

    lax.fori_loop(0, out_ref.shape[0], one_row, 0)


def assemble(me, blocks):
    rows, height, lanes = blocks[0].shape
    return pl.pallas_call(
        assemble_kernel,
        in_specs=[smem] + [vmem] * len(blocks),
        out_specs=vmem,
        out_shape=jax.ShapeDtypeStruct((rows, height * len(blocks), lanes), bf16),
        scratch_shapes=[pltpu.VMEM((lanes // 128, height * len(blocks), 128), f32)],
        compiler_params=pltpu.CompilerParams(vmem_limit_bytes=VMEM_LIMIT),
        name="assemble",
    )(me, *blocks)


def central(first, second, fourth, fifth):
    return ((first - 8.0 * second + 8.0 * fourth - fifth) / 12.0).astype(bf16)


def galerkin_kernel(plan, has_sum, rows_y, *refs):
    runs, field_plan, halo_plan = plan
    count = len(halo_plan)
    stride = 3 if runs > 1 else 1
    refs = list(refs)
    conv_in, diss_in = (refs.pop(0), refs.pop(0)) if has_sum else (None, None)
    volume_ref = refs.pop(0)
    fields, low, high, slopes_ref, values, stationary, carried, volumes = refs[-8:]
    conv_ref, diss_ref = refs[-10:-8]
    sources = refs[:-10]
    for slot, (operand, row) in enumerate(field_plan):
        fields[slot] = sources[operand][row]
    for slot, (low_operand, high_operand, row, cell_row) in enumerate(halo_plan):
        low[slot] = sources[low_operand][row]
        high[slot] = sources[high_operand][row]
        volumes[slot] = volume_ref[cell_row]
    if has_sum:
        conv_ref[...] = conv_in[...]
        diss_ref[...] = diss_in[...]
    else:
        conv_ref[...] = jnp.zeros_like(conv_ref)
        diss_ref[...] = jnp.zeros_like(diss_ref)

    height, lanes = fields.shape[1:]
    half = height // 2
    mode_count = half // 3
    row_y = lax.broadcasted_iota(jnp.int32, (height, lanes), 1) % rows_y

    def shifted(array, step):
        moved = pltpu.roll(array, (-step) % lanes, 1)
        inside = (row_y + step >= 0) & (row_y + step < rows_y)
        return jnp.where(inside, moved, 0.0)

    def one_step(step, unused):
        base = step * stride
        before = fields[base].astype(f32)
        here = fields[base + 1].astype(f32)
        after = fields[base + 2].astype(f32)
        left = low[step].astype(f32)
        right = high[step].astype(f32)
        along_x = central(
            left,
            jnp.concatenate([left[:, rows_y:], here[:, : lanes - rows_y]], axis=1),
            jnp.concatenate([here[:, rows_y:], right[:, : lanes - rows_y]], axis=1),
            right,
        )
        along_y = central(shifted(here, -2), shifted(here, -1), shifted(here, 1), shifted(here, 2))
        along_z = jnp.concatenate(
            [
                central(before[:half], before[half:], here[half:], after[:half]),
                central(before[half:], here[:half], after[:half], after[half:]),
            ],
            axis=0,
        )
        weights = volumes[step]
        weighted = []
        for parity in range(2):
            span = pl.ds(parity * lanes, lanes)
            values[:, span] = fields[base + 1, parity * half : (parity + 1) * half, :]
            product = here[parity * half : (parity + 1) * half] * weights[parity : parity + 1]
            coarse = product.astype(bf16)
            fine = (product - coarse.astype(f32)).astype(bf16)
            for comp in range(3):
                rows = slice(comp * mode_count, (comp + 1) * mode_count)
                place = pl.ds((2 * comp + parity) * lanes, lanes)
                stationary[:mode_count, place] = coarse[rows]
                stationary[mode_count:, place] = fine[rows]
        for comp in range(3):
            for direction, along in enumerate((along_x, along_y, along_z)):
                pieces = [
                    along[parity * half + comp * mode_count : parity * half + (comp + 1) * mode_count]
                    for parity in range(2)
                ]
                number = comp * 3 + direction
                for parity in range(2):
                    slopes_ref[
                        number * mode_count : (number + 1) * mode_count,
                        parity * lanes : (parity + 1) * lanes,
                    ] = pieces[parity]
                    scaled = pieces[parity].astype(f32) * weights[parity : parity + 1]
                    weighted.append(scaled.astype(bf16))
        diss_ref[...] += sum(
            lax.dot_general(
                slopes_ref[number * mode_count : (number + 1) * mode_count, :],
                jnp.concatenate(weighted[2 * number : 2 * number + 2], axis=1),
                (((1,), (1,)), ((), ())),
                preferred_element_type=f32,
            )
            for number in range(9)
        )
        width = 2 * lanes
        for j in range(mode_count):
            rows = [
                jnp.broadcast_to(
                    values[b * mode_count + j : b * mode_count + j + 1, :], (mode_count, width)
                )
                for b in range(3)
            ]
            for a in range(3):
                slopes = [
                    slopes_ref[(a * 3 + b) * mode_count : (a * 3 + b + 1) * mode_count, :]
                    for b in range(3)
                ]
                total = rows[0] * slopes[0] + rows[1] * slopes[1] + rows[2] * slopes[2]
                carried[j * mode_count : (j + 1) * mode_count, a * width : (a + 1) * width] = total
        conv_ref[...] += lax.dot_general(
            carried[...], stationary[...], (((1,), (1,)), ((), ())), preferred_element_type=f32
        )
        return unused

    lax.fori_loop(0, count, one_step, 0)


def galerkin(sums, volume, sources, plan, rows_y):
    runs, field_plan, halo_plan = plan
    height, lanes = sources[0].shape[1:]
    mode_count = height // 6
    operands = list(sums or ()) + [volume] + list(sources)
    return pl.pallas_call(
        functools.partial(galerkin_kernel, plan, sums is not None, rows_y),
        in_specs=[vmem] * len(operands),
        out_specs=(vmem, vmem),
        out_shape=(
            jax.ShapeDtypeStruct((mode_count * mode_count, 2 * mode_count), f32),
            jax.ShapeDtypeStruct((mode_count, mode_count), f32),
        ),
        scratch_shapes=[
            pltpu.VMEM((len(field_plan), height, lanes), bf16),
            pltpu.VMEM((len(halo_plan), height, lanes), bf16),
            pltpu.VMEM((len(halo_plan), height, lanes), bf16),
            pltpu.VMEM((9 * mode_count, 2 * lanes), bf16),
            pltpu.VMEM((3 * mode_count, 2 * lanes), bf16),
            pltpu.VMEM((2 * mode_count, 6 * lanes), bf16),
            pltpu.VMEM((mode_count * mode_count, 6 * lanes), bf16),
            pltpu.VMEM((len(halo_plan), 2, lanes), f32),
        ],
        compiler_params=pltpu.CompilerParams(vmem_limit_bytes=VMEM_LIMIT),
        name="galerkin",
    )(*operands)


def local_volume(volume, planes, cells_z):
    slabs = lax.axis_size("slab")
    owners = lax.axis_size("mode")
    rows = volume.shape[1]
    split = volume.reshape(slabs, planes, rows, owners, cells_z).transpose(3, 0, 4, 1, 2)
    split = split.reshape(owners * slabs, cells_z * planes * rows)
    moved = lax.all_to_all(split, ("mode", "slab"), 0, 0, tiled=True)
    moved = moved.reshape(owners * slabs, cells_z, planes, rows).transpose(1, 2, 0, 3)
    return moved.reshape(cells_z // 2, 2, planes * owners * slabs * rows)


def per_device(modes, volume):
    local, comps, planes, rows_y, cells = modes.shape
    owners = lax.axis_size("mode")
    slabs = lax.axis_size("slab")
    devices = owners * slabs
    mode_count = local * owners
    lanes = planes * rows_y
    pairs = cells // 2 // owners
    me = lax.axis_index("mode")
    me_word = me.astype(jnp.int32).reshape(1)

    turned = modes.transpose(4, 1, 0, 2, 3).reshape(cells // 2, 2 * comps * local, lanes)
    first = int(pairs * FIRST)
    spans = ((0, first), (first, pairs))

    def row_of(target, row):
        return lax.rem(target * pairs + row + cells // 2, cells // 2)

    def take(target, chunk):
        if chunk < 2:
            start, stop = spans[chunk]
            return lax.dynamic_slice_in_dim(turned, target * pairs + start, stop - start, 0)
        return jnp.concatenate(
            [
                lax.dynamic_slice_in_dim(turned, row_of(target, row), 1, 0)
                for row in (-1, pairs)
            ],
            axis=0,
        )

    fields = []
    for chunk in range(3):
        blocks = [take(me, chunk)]
        for shift in range(1, owners):
            exchange = [(source, source ^ shift) for source in range(owners)]
            blocks.append(lax.ppermute(take(me ^ shift, chunk), "mode", exchange))
        fields.append(assemble(me_word, blocks))
    weights = local_volume(volume, planes, cells // owners)

    forward = [(source, source + 1) for source in range(slabs - 1)]
    backward = [(target, source) for source, target in forward]
    lows = [lax.ppermute(fields[chunk], "slab", forward) for chunk in range(2)]
    highs = [lax.ppermute(fields[chunk], "slab", backward) for chunk in range(2)]

    def place(row):
        if row < 0:
            return (2, 0)
        if row >= pairs:
            return (2, 1)
        return (0, row) if row < first else (1, row - first)

    def plan_of(runs):
        field_plan, halo_plan = [], []
        for start, stop in runs:
            field_plan += [place(row) for row in range(start - 1, stop + 1)]
            for row in range(start, stop):
                chunk, inner = place(row)
                halo_plan.append((3 + chunk, 5 + chunk, inner, row))
        return (len(runs), field_plan, halo_plan)

    def compact(plan, sources):
        runs, field_plan, halo_plan = plan
        used = sorted(
            {entry[0] for entry in field_plan}
            | {entry[0] for entry in halo_plan}
            | {entry[1] for entry in halo_plan}
        )
        number = {operand: place for place, operand in enumerate(used)}
        field_plan = tuple((number[operand], row) for operand, row in field_plan)
        halo_plan = tuple((number[p], number[q], row, cell) for p, q, row, cell in halo_plan)
        return [sources[operand] for operand in used], (runs, field_plan, halo_plan)

    sources = fields + lows + highs
    sums = None
    for runs in ([(1, first - 1)], [(first - 1, pairs - 1)], [(pairs - 1, pairs), (0, 1)]):
        chosen, plan = compact(plan_of(runs), sources)
        sums = galerkin(sums, weights, chosen, plan, rows_y)
    conv, diss = sums
    conv = conv[:, :mode_count] + conv[:, mode_count:]

    share = mode_count**3 // devices
    padded = -(-share // 128) * 128
    conv = conv.T.reshape(devices, share)
    conv = jnp.pad(conv, ((0, 0), (0, padded - share))).reshape(devices, padded // 128, 128)
    extra = jnp.broadcast_to(
        diss.reshape(1, mode_count * mode_count // 128, 128), (devices, mode_count**2 // 128, 128)
    )
    packed = jnp.concatenate([conv, extra], axis=1).astype(bf16)
    moved = lax.all_to_all(packed, ("mode", "slab"), 0, 0, tiled=True)
    summed = moved.astype(f32).sum(0)
    total_cells = cells * rows_y * planes * slabs
    convective = summed[: padded // 128].reshape(padded)[:share].reshape(-1, mode_count)
    dissipation = summed[padded // 128 :].reshape(mode_count, mode_count)
    return (
        convective * (1.0 / math.sqrt(total_cells)),
        dissipation * (viscosity / total_cells),
    )


def solution(mesh):
    placed = (P("mode", None, "slab", None, None), P(None, ("mode", "slab"), None))
    return jax.shard_map(
        per_device,
        mesh=mesh,
        in_specs=placed,
        out_specs=(P(("mode", "slab"), None), P()),
        check_vma=False,
    )
```

time: 562 us -> 131 us (0.23)
  blocking collectives: 144 us -> 18.5 us
  local copies, waits for them, and re-layouts: 114 us -> 16.3 us
  waiting for transfers between devices: 110 us -> 12.9 us
  other arithmetic: 94.4 us -> 2.83 us
  matrix products: 48.7 us -> 0 us
  Pallas kernels: 0 us -> 39.1 us
  between operations: 14.2 us -> 1.03 us
    all_to_all x1, blocking collectives: 105 us -> 18.5 us  [per_device(): moved = lax.all_to_all(packed, ('mode', 'slab'), 0, 0, tiled=True)]
    convert_element_type x8 -> x0, other arithmetic: 85 us -> none  [the longest x4 79.5 us: one_step(): carried = (carried * piece_weights).astype(jnp.bfloat16).reshape(mode_cou...]
    unnamed x2 -> x0, waiting for transfers between devices: 55.2 us -> none
    all_to_all x1, waiting for transfers between devices: 54.8 us -> 0.01 us  [local_volume(): moved = lax.all_to_all(split, ('mode', 'slab'), 0, 0, tiled=True)]
    dot_general x8 -> x0, matrix products: 48.7 us -> none  [the longest x4 41 us: one_step(): lax.dot_general(piece_values.reshape(mode_count, 3 * block_size), carried...]
    while x32 -> x0, local copies, waits for them, and re-layouts: 45 us -> none
    pallas_call x0 -> x6, Pallas kernels: none -> 39.1 us  [the longest x3 33.3 us: galerkin(): pl.pallas_call(functools.partial(galerkin_kernel, plan, sums is not None,...]
    psum x1 -> x0, blocking collectives: 38.1 us -> none  [per_device(): diss_sum = lax.psum(diss_part, ('mode', 'slab'))]
  transfers between devices with their start and end apart: 4 -> 14, of which waited for: 3 -> 4; matrix products, arithmetic and copies ran while one was open for 1% -> 3% of each run, Pallas kernels for 0% -> 13%
where the time goes in v1:
time: 131 us
  starting transfers between devices  40.3 us (31%)
  Pallas kernels  39.1 us (30%)
  blocking collectives  18.5 us (14%)
  local copies, waits for them, and re-layouts  16.3 us (12%)
  waiting for transfers between devices  12.9 us (10%)
  other arithmetic  2.83 us (2%)
    pallas_call x3, Pallas kernels, galerkin(): pl.pallas_call(functools.partial(galerkin_kernel, plan, sums is not None,...  33.3 us
    ppermute x9, starting transfers between devices, per_device(): blocks.append(lax.ppermute(take(me ^ shift, chunk), 'mode', exchange))  24.8 us
    all_to_all x1, blocking collectives, per_device(): moved = lax.all_to_all(packed, ('mode', 'slab'), 0, 0, tiled=True)  18.5 us
    ppermute x9, waiting for transfers between devices, per_device(): blocks.append(lax.ppermute(take(me ^ shift, chunk), 'mode', exchange))  12.8 us
    ppermute x2, starting transfers between devices, per_device(): lows = [lax.ppermute(fields[chunk], 'slab', forward) for chunk in range(2)]  7.49 us
    pallas_call x3, Pallas kernels, assemble(): pl.pallas_call(assemble_kernel, in_specs=[smem] + [vmem] * len(blocks), o...  5.82 us
    transpose x1, local copies, waits for them, and re-layouts, per_device(): modes.transpose(4, 1, 0, 2, 3).reshape(cells // 2, 2 * comps * local, lanes)  5.66 us
    all_to_all x1, starting transfers between devices, local_volume(): moved = lax.all_to_all(split, ('mode', 'slab'), 0, 0, tiled=True)  5.45 us
  transfers between devices with their start and end apart: 14, of which 4 were waited for; matrix products, arithmetic and copies ran while one was open for 3% of the time, Pallas kernels for 13%

profile of v1, /device:TPU:0, one launch (start us, length us, event | category | flops | bytes accessed | tf_op | source)
XLA Modules:
  0.0 130.9 jit_solution(4915417657706291903)
XLA Ops:
  0.7 5.7 %copy.14 = bf16[128,3,12,2,64]{4,3,2,1,0:T(2,128)(2,1)S(1)} copy(bf16[128,3,12,2,64]{0,4,3,1,2:T(8,128)(2,1)} %bitcast.12) | data formatting | bytes 2359296 | tf_op jit(solution)/shard_map/transpose | solution.py:222
  6.3 1.1 reshape.41
  7.5 0.8 constant_dynamic-slice_fusion.8
  8.3 5.0 %collective-permute-start.2 = (bf16[8,72,128]{2,1,0:T(8,128)(2,1)S(1)}, bf16[8,72,128]{2,1,0:T(8,128)(2,1)S(1)}, u32[]{:S(2)}, u32[]{:S(2)}) collective-permute-start(bf16[8,72,128]{2,1,0:T(8,128)(2,1)S(1)} %get-tuple-element.30), channel_id=1, source_target_pairs={{0,24},{8,16},{16,8},{24,0},{1,25},{9,17},{17,9},{25,1},{2,26},{10... | collective-permute-start | bytes 442376 | tf_op jit(solution)/shard_map/ppermute | solution.py:246
  13.3 0.0 collective-permute-start.1
  13.3 0.6 collective-permute-start
  13.9 3.8 %collective-permute-start.7 = (bf16[8,72,128]{2,1,0:T(8,128)(2,1)S(1)}, bf16[8,72,128]{2,1,0:T(8,128)(2,1)S(1)}, u32[]{:S(2)}, u32[]{:S(2)}) collective-permute-start(bf16[8,72,128]{2,1,0:T(8,128)(2,1)S(1)} %get-tuple-element.26), channel_id=1, source_target_pairs={{0,24},{8,16},{16,8},{24,0},{1,25},{9,17},{17,9},{25,1},{2,26},{10... | collective-permute-start | bytes 442376 | tf_op jit(solution)/shard_map/ppermute | solution.py:246
  17.7 0.0 collective-permute-start.6
  17.7 0.4 collective-permute-done.2.refs_3_
  18.1 6.9 %collective-permute-start.5 = (bf16[8,72,128]{2,1,0:T(8,128)(2,1)S(1)}, bf16[8,72,128]{2,1,0:T(8,128)(2,1)S(1)}, u32[]{:S(2)}, u32[]{:S(2)}) collective-permute-start(bf16[8,72,128]{2,1,0:T(8,128)(2,1)S(1)} %get-tuple-element.28), channel_id=1, source_target_pairs={{0,8},{8,0},{16,24},{24,16},{1,9},{9,1},{17,25},{25,17},{2,10},{10... | collective-permute-start | bytes 442376 | tf_op jit(solution)/shard_map/ppermute | solution.py:246
  25.0 8.1 %collective-permute-done.1.refs_2_ = bf16[8,72,128]{2,1,0:T(8,128)(2,1)S(1)} collective-permute-done((bf16[8,72,128]{2,1,0:T(8,128)(2,1)S(1)}, bf16[8,72,128]{2,1,0:T(8,128)(2,1)S(1)}, u32[]{:S(2)}, u32[]{:S(2)}) %collective-permute-start.1) | collective-permute-done | bytes 147488 | tf_op jit(solution)/shard_map/ppermute | solution.py:246
  33.1 0.0 collective-permute-done.refs_1_
  33.1 0.7 copy-done.6
  33.8 0.0 copy-done.7
  33.8 2.1 %assemble.3.refs_1_.refs_3_ = bf16[8,288,128]{2,1,0:T(8,128)(2,1)} custom-call(s32[1]{0:T(128)} %bitcast.3.me_ref, bf16[8,72,128]{2,1,0:T(8,128)(2,1)} %get-tuple-element.33.refs_0_, bf16[8,72,128]{2,1,0:T(8,128)(2,1)} %copy-done.7, bf16[8,72,128]{2,1,0:T(8,128)(2,1)} %copy-done.6, bf16[8,72,128]{2,1,0:T(8,128)(2,1)} %copy-done.5), custom_call_target="tpu_custom_call" | custom-call | tf_op jit(solution)/shard_map/assemble/pallas_call | solution.py:44
  36.0 1.3 collective-permute-start.4
  37.3 3.1 %collective-permute-start.3 = (bf16[8,288,128]{2,1,0:T(8,128)(2,1)}, bf16[8,288,128]{2,1,0:T(8,128)(2,1)S(1)}, u32[]{:S(2)}, u32[]{:S(2)}) collective-permute-start(bf16[8,288,128]{2,1,0:T(8,128)(2,1)} %assemble.3.refs_1_.refs_3_), channel_id=1, source_target_pairs={{0,1},{1,2},{2,3},{3,4},{4,5},{5,6},{6,7},{8,9},{9,10},{10,11},{11... | collective-permute-start | bytes 1769480 | tf_op jit(solution)/shard_map/ppermute | solution.py:252
  40.3 0.0 collective-permute-done.7.refs_3_
  40.3 0.0 collective-permute-done.6.refs_2_
  40.4 0.0 collective-permute-done.5.refs_1_
  40.4 0.0 copy-start.4
  40.4 0.6 copy-done.2
  41.0 0.0 copy-done.3
  41.1 0.1 copy-done.4
  41.1 2.1 %assemble.4.refs_4_ = bf16[8,288,128]{2,1,0:T(8,128)(2,1)} custom-call(s32[1]{0:T(128)} %bitcast.3.me_ref, bf16[8,72,128]{2,1,0:T(8,128)(2,1)} %get-tuple-element.29.refs_0_, bf16[8,72,128]{2,1,0:T(8,128)(2,1)} %copy-done.4, bf16[8,72,128]{2,1,0:T(8,128)(2,1)} %copy-done.3, bf16[8,72,128]{2,1,0:T(8,128)(2,1)} %copy-done.2), custom_call_target="tpu_custom_call" | custom-call | tf_op jit(solution)/shard_map/assemble/pallas_call | solution.py:44
  43.2 1.3 collective-permute-start.9
  44.5 4.4 %collective-permute-start.8 = (bf16[8,288,128]{2,1,0:T(8,128)(2,1)}, bf16[8,288,128]{2,1,0:T(8,128)(2,1)}, u32[]{:S(2)}, u32[]{:S(2)}) collective-permute-start(bf16[8,288,128]{2,1,0:T(8,128)(2,1)} %assemble.4.refs_4_), channel_id=1, source_target_pairs={{0,1},{1,2},{2,3},{3,4},{4,5},{5,6},{6,7},{8,9},{9,10},{10,11},{11... | collective-permute-start | bytes 1769480 | tf_op jit(solution)/shard_map/ppermute | solution.py:252
  49.0 0.1 reshape.37
  49.1 0.2 copy.10
  49.3 0.2 all_to_all.9
  49.4 0.7 copy.11
  50.1 5.5 %all-to-all-start = ((f32[32,1,128]{2,1,0:T(1,128)}), f32[32,1,128]{2,1,0:T(1,128)S(1)}, u32[]{:S(2)}, u32[]{:S(2)}) async-start(f32[32,1,128]{2,1,0:T(1,128)} %copy.11), calls=%async_computation | async-start | bytes 32768 | tf_op jit(solution)/shard_map/all_to_all | solution.py:206
  55.7 1.8 %collective-permute-start.10 = (bf16[2,72,128]{2,1,0:T(8,128)(2,1)S(1)}, bf16[2,72,128]{2,1,0:T(8,128)(2,1)S(1)}, u32[]{:S(2)}, u32[]{:S(2)}) collective-permute-start(bf16[2,72,128]{2,1,0:T(8,128)(2,1)S(1)} %pad_maximum_fusion.2), channel_id=1, source_target_pairs={{0,8},{8,0},{16,24},{24,16},{1,9},{9,1},{17,25},{25,17},{2,10},{10... | collective-permute-start | bytes 110600 | tf_op jit(solution)/shard_map/ppermute | solution.py:246
  57.6 2.2 %collective-permute-done.10.refs_1_ = bf16[2,72,128]{2,1,0:T(8,128)(2,1)S(1)} collective-permute-done((bf16[2,72,128]{2,1,0:T(8,128)(2,1)S(1)}, bf16[2,72,128]{2,1,0:T(8,128)(2,1)S(1)}, u32[]{:S(2)}, u32[]{:S(2)}) %collective-permute-start.10) | collective-permute-done | bytes 36896 | tf_op jit(solution)/shard_map/ppermute | solution.py:246
  59.8 2.7 %collective-permute-start.11 = (bf16[2,72,128]{2,1,0:T(8,128)(2,1)S(1)}, bf16[2,72,128]{2,1,0:T(8,128)(2,1)S(1)}, u32[]{:S(2)}, u32[]{:S(2)}) collective-permute-start(bf16[2,72,128]{2,1,0:T(8,128)(2,1)S(1)} %pad_maximum_fusion.3), channel_id=1, source_target_pairs={{0,16},{8,24},{16,0},{24,8},{1,17},{9,25},{17,1},{25,9},{2,18},{10... | collective-permute-start | bytes 110600 | tf_op jit(solution)/shard_map/ppermute | solution.py:246
  62.4 2.2 %collective-permute-done.11.refs_2_ = bf16[2,72,128]{2,1,0:T(8,128)(2,1)S(1)} collective-permute-done((bf16[2,72,128]{2,1,0:T(8,128)(2,1)S(1)}, bf16[2,72,128]{2,1,0:T(8,128)(2,1)S(1)}, u32[]{:S(2)}, u32[]{:S(2)}) %collective-permute-start.11) | collective-permute-done | bytes 36896 | tf_op jit(solution)/shard_map/ppermute | solution.py:246
  64.6 4.0 %collective-permute-start.12 = (bf16[2,72,128]{2,1,0:T(8,128)(2,1)S(1)}, bf16[2,72,128]{2,1,0:T(8,128)(2,1)S(1)}, u32[]{:S(2)}, u32[]{:S(2)}) collective-permute-start(bf16[2,72,128]{2,1,0:T(8,128)(2,1)S(1)} %pad_maximum_fusion.4), channel_id=1, source_target_pairs={{0,24},{8,16},{16,8},{24,0},{1,25},{9,17},{17,9},{25,1},{2,26},{10... | collective-permute-start | bytes 110600 | tf_op jit(solution)/shard_map/ppermute | solution.py:246
  68.6 0.6 pad_maximum_fusion.1.refs_0_
  69.2 0.0 all-to-all-done
  69.2 0.1 copy.12
  69.3 0.5 copy.13
  69.8 1.2 reshape.39.refs_0_.refs_2_
  71.0 0.0 collective-permute-done.12.refs_3_
  71.0 0.6 copy-done.10
  71.6 1.5 %assemble.5.refs_5_ = bf16[2,288,128]{2,1,0:T(8,128)(2,1)} custom-call(s32[1]{0:T(128)} %bitcast.3.me_ref, bf16[2,72,128]{2,1,0:T(8,128)(2,1)} %pad_maximum_fusion.1.refs_0_, bf16[2,72,128]{2,1,0:T(8,128)(2,1)} %copy-done.8, bf16[2,72,128]{2,1,0:T(8,128)(2,1)} %copy-done.9, bf16[2,72,128]{2,1,0:T(8,128)(2,1)} %copy-done.10), custom_call_target="tpu_custom_call" | custom-call | tf_op jit(solution)/shard_map/assemble/pallas_call | solution.py:44
  73.1 0.0 collective-permute-done.4.refs_3_.refs_7_.refs_8_
  73.1 0.0 collective-permute-done.3.refs_2_.refs_5_.refs_6_
  73.1 0.8 copy-done
  73.9 0.8 copy-done.1
  74.8 11.4 %galerkin.3 = (f32[2304,96]{1,0:T(8,128)}, f32[48,48]{1,0:T(8,128)}) custom-call(f32[16,2,128]{2,1,0:T(2,128)} %reshape.39.refs_0_.refs_2_, bf16[8,288,128]{2,1,0:T(8,128)(2,1)} %assemble.3.refs_1_.refs_3_, bf16[8,288,128]{2,1,0:T(8,128)(2,1)} %copy-done.1, bf16[8,288,128]{2,1,0:T(8,128)(2,1)} %copy-done), custom_call_target="tpu_custom_call" | custom-call | tf_op jit(solution)/shard_map/galerkin/pallas_call | solution.py:177
  86.2 0.0 collective-permute-done.9.refs_8_.refs_9_
  86.2 0.0 collective-permute-done.8.refs_6_.refs_7_
  86.2 15.4 %galerkin.4 = (f32[2304,96]{1,0:T(8,128)}, f32[48,48]{1,0:T(8,128)}) custom-call(f32[2304,96]{1,0:T(8,128)} %get-tuple-element.8.refs_0_, f32[48,48]{1,0:T(8,128)} %get-tuple-element.9.refs_1_, f32[16,2,128]{2,1,0:T(2,128)} %reshape.39.refs_0_.refs_2_, bf16[8,288,128]{2,1,0:T(8,128)(2,1)} %assemble.3.refs_1_.refs_3_, bf16[8,288,128]{2,1,0:T(8,128)(2,1)} %assemble.4.refs_4_, ...), custom_call_target="tpu_custom_call" | custom-call | tf_op jit(solution)/shard_map/galerkin/pallas_call | solution.py:177
  101.6 6.5 %galerkin.5 = (f32[2304,96]{1,0:T(8,128)}, f32[48,48]{1,0:T(8,128)}) custom-call(f32[2304,96]{1,0:T(8,128)} %get-tuple-element.10.refs_0_, f32[48,48]{1,0:T(8,128)} %get-tuple-element.11.refs_1_, f32[16,2,128]{2,1,0:T(2,128)} %reshape.39.refs_0_.refs_2_, bf16[8,288,128]{2,1,0:T(8,128)(2,1)} %assemble.3.refs_1_.refs_3_, ...), custom_call_target="tpu_custom_call" | custom-call | tf_op jit(solution)/shard_map/galerkin/pallas_call | solution.py:177
  108.1 2.0 %fusion = bf16[48,2304]{0,1:T(8,128)(2,1)S(1)} fusion(f32[2304,96]{1,0:T(8,128)} %get-tuple-element.12), kind=kLoop, calls=%fused_computation.2 | loop fusion | flops 221184 | bytes 1105920 | tf_op jit(solution)/shard_map/transpose | solution.py:293
  110.1 0.2 copy.15
  110.3 0.1 reshape.43
  110.4 0.3 reshape.42
  110.7 0.1 pad_maximum_fusion
  110.8 18.5 %all_to_all.14 = bf16[32,45,128]{2,1,0:T(8,128)(2,1)S(1)} all-to-all(bf16[32,45,128]{2,1,0:T(8,128)(2,1)S(1)} %pad_maximum_fusion), channel_id=1, replica_groups=mesh['mode'=4,'slab'=8] {'mode','slab'}, dimensions={0} | all-to-all | bytes 737280 | tf_op jit(solution)/shard_map/all_to_all | solution.py:299
  129.4 0.1 convert_reduce_fusion
  129.5 0.7 mul.51
  130.2 0.1 mul.48
  130.3 0.7 copy.16
  (25 shorter events, 0.1 us)
Async XLA Ops:
  8.3 9.8 %collective-permute-start.2 = (bf16[8,72,128]{2,1,0:T(8,128)(2,1)S(1)}, bf16[8,72,128]{2,1,0:T(8,128)(2,1)S(1)}, u32[]{:S(2)}, u32[]{:S(2)}) collective-permute-start(bf16[8,72,128]{2,1,0:T(8,128)(2,1)S(1)} %get-tuple-element.30), channel_id=1, source_target_pairs={{0,24},{8,16},{16,8},{24,0},{1,25},{9,17},{17,9},{25,1},{2,26},{10... | collective-permute-start | bytes 442376 | tf_op jit(solution)/shard_map/ppermute | solution.py:246
  13.3 19.8 %collective-permute-start.1 = (bf16[8,72,128]{2,1,0:T(8,128)(2,1)S(1)}, bf16[8,72,128]{2,1,0:T(8,128)(2,1)S(1)}, u32[]{:S(2)}, u32[]{:S(2)}) collective-permute-start(bf16[8,72,128]{2,1,0:T(8,128)(2,1)S(1)} %get-tuple-element.31), channel_id=1, source_target_pairs={{0,16},{8,24},{16,0},{24,8},{1,17},{9,25},{17,1},{25,9},{2,18},{10... | collective-permute-start | bytes 442376 | tf_op jit(solution)/shard_map/ppermute | solution.py:246
  13.3 19.8 %collective-permute-start = (bf16[8,72,128]{2,1,0:T(8,128)(2,1)S(1)}, bf16[8,72,128]{2,1,0:T(8,128)(2,1)S(1)}, u32[]{:S(2)}, u32[]{:S(2)}) collective-permute-start(bf16[8,72,128]{2,1,0:T(8,128)(2,1)S(1)} %get-tuple-element.32), channel_id=1, source_target_pairs={{0,8},{8,0},{16,24},{24,16},{1,9},{9,1},{17,25},{25,17},{2,10},{10... | collective-permute-start | bytes 442376 | tf_op jit(solution)/shard_map/ppermute | solution.py:246
  13.9 26.4 %collective-permute-start.7 = (bf16[8,72,128]{2,1,0:T(8,128)(2,1)S(1)}, bf16[8,72,128]{2,1,0:T(8,128)(2,1)S(1)}, u32[]{:S(2)}, u32[]{:S(2)}) collective-permute-start(bf16[8,72,128]{2,1,0:T(8,128)(2,1)S(1)} %get-tuple-element.26), channel_id=1, source_target_pairs={{0,24},{8,16},{16,8},{24,0},{1,25},{9,17},{17,9},{25,1},{2,26},{10... | collective-permute-start | bytes 442376 | tf_op jit(solution)/shard_map/ppermute | solution.py:246
  17.7 22.6 %collective-permute-start.6 = (bf16[8,72,128]{2,1,0:T(8,128)(2,1)S(1)}, bf16[8,72,128]{2,1,0:T(8,128)(2,1)S(1)}, u32[]{:S(2)}, u32[]{:S(2)}) collective-permute-start(bf16[8,72,128]{2,1,0:T(8,128)(2,1)S(1)} %get-tuple-element.27), channel_id=1, source_target_pairs={{0,16},{8,24},{16,0},{24,8},{1,17},{9,25},{17,1},{25,9},{2,18},{10... | collective-permute-start | bytes 442376 | tf_op jit(solution)/shard_map/ppermute | solution.py:246
  18.1 15.0 %copy-start.5 = (bf16[8,72,128]{2,1,0:T(8,128)(2,1)}, bf16[8,72,128]{2,1,0:T(8,128)(2,1)S(1)}, u32[]{:S(2)}) copy-start(bf16[8,72,128]{2,1,0:T(8,128)(2,1)S(1)} %collective-permute-done.2.refs_3_) | copy-start | bytes 442372
  18.1 22.3 %collective-permute-start.5 = (bf16[8,72,128]{2,1,0:T(8,128)(2,1)S(1)}, bf16[8,72,128]{2,1,0:T(8,128)(2,1)S(1)}, u32[]{:S(2)}, u32[]{:S(2)}) collective-permute-start(bf16[8,72,128]{2,1,0:T(8,128)(2,1)S(1)} %get-tuple-element.28), channel_id=1, source_target_pairs={{0,8},{8,0},{16,24},{24,16},{1,9},{9,1},{17,25},{25,17},{2,10},{10... | collective-permute-start | bytes 442376 | tf_op jit(solution)/shard_map/ppermute | solution.py:246
  33.1 0.7 copy-start.6
  33.1 0.7 copy-start.7
  33.8 15.1 %copy-start.12 = (f32[16,2,128]{2,1,0:T(2,128)S(1)}, f32[16,2,128]{2,1,0:T(2,128)}, u32[]{:S(2)}) copy-start(f32[16,2,128]{2,1,0:T(2,128)} %param.3) | copy-start | bytes 49156
  36.0 37.2 %collective-permute-start.4 = (bf16[8,288,128]{2,1,0:T(8,128)(2,1)}, bf16[8,288,128]{2,1,0:T(8,128)(2,1)S(1)}, u32[]{:S(2)}, u32[]{:S(2)}) collective-permute-start(bf16[8,288,128]{2,1,0:T(8,128)(2,1)} %assemble.3.refs_1_.refs_3_), channel_id=1, source_target_pairs={{1,0},{2,1},{3,2},{4,3},{5,4},{6,5},{7,6},{9,8},{10,9},{11,10},{12... | collective-permute-start | bytes 1769480 | tf_op jit(solution)/shard_map/ppermute | solution.py:253
  37.3 35.9 %collective-permute-start.3 = (bf16[8,288,128]{2,1,0:T(8,128)(2,1)}, bf16[8,288,128]{2,1,0:T(8,128)(2,1)S(1)}, u32[]{:S(2)}, u32[]{:S(2)}) collective-permute-start(bf16[8,288,128]{2,1,0:T(8,128)(2,1)} %assemble.3.refs_1_.refs_3_), channel_id=1, source_target_pairs={{0,1},{1,2},{2,3},{3,4},{4,5},{5,6},{6,7},{8,9},{9,10},{10,11},{11... | collective-permute-start | bytes 1769480 | tf_op jit(solution)/shard_map/ppermute | solution.py:252
  40.3 0.7 copy-start.2
  40.4 0.7 copy-start.3
  40.4 0.7 copy-start.4
  43.2 43.0 %collective-permute-start.9 = (bf16[8,288,128]{2,1,0:T(8,128)(2,1)}, bf16[8,288,128]{2,1,0:T(8,128)(2,1)}, u32[]{:S(2)}, u32[]{:S(2)}) collective-permute-start(bf16[8,288,128]{2,1,0:T(8,128)(2,1)} %assemble.4.refs_4_), channel_id=1, source_target_pairs={{1,0},{2,1},{3,2},{4,3},{5,4},{6,5},{7,6},{9,8},{10,9},{11,10},{12... | collective-permute-start | bytes 1769480 | tf_op jit(solution)/shard_map/ppermute | solution.py:253
  44.5 41.7 %collective-permute-start.8 = (bf16[8,288,128]{2,1,0:T(8,128)(2,1)}, bf16[8,288,128]{2,1,0:T(8,128)(2,1)}, u32[]{:S(2)}, u32[]{:S(2)}) collective-permute-start(bf16[8,288,128]{2,1,0:T(8,128)(2,1)} %assemble.4.refs_4_), channel_id=1, source_target_pairs={{0,1},{1,2},{2,3},{3,4},{4,5},{5,6},{6,7},{8,9},{9,10},{10,11},{11... | collective-permute-start | bytes 1769480 | tf_op jit(solution)/shard_map/ppermute | solution.py:252
  50.1 19.1 %all-to-all-start = ((f32[32,1,128]{2,1,0:T(1,128)}), f32[32,1,128]{2,1,0:T(1,128)S(1)}, u32[]{:S(2)}, u32[]{:S(2)}) async-start(f32[32,1,128]{2,1,0:T(1,128)} %copy.11), calls=%async_computation | async-start | bytes 32768 | tf_op jit(solution)/shard_map/all_to_all | solution.py:206
  55.7 4.0 %collective-permute-start.10 = (bf16[2,72,128]{2,1,0:T(8,128)(2,1)S(1)}, bf16[2,72,128]{2,1,0:T(8,128)(2,1)S(1)}, u32[]{:S(2)}, u32[]{:S(2)}) collective-permute-start(bf16[2,72,128]{2,1,0:T(8,128)(2,1)S(1)} %pad_maximum_fusion.2), channel_id=1, source_target_pairs={{0,8},{8,0},{16,24},{24,16},{1,9},{9,1},{17,25},{25,17},{2,10},{10... | collective-permute-start | bytes 110600 | tf_op jit(solution)/shard_map/ppermute | solution.py:246
  59.8 11.2 %copy-start.8 = (bf16[2,72,128]{2,1,0:T(8,128)(2,1)}, bf16[2,72,128]{2,1,0:T(8,128)(2,1)S(1)}, u32[]{:S(2)}) copy-start(bf16[2,72,128]{2,1,0:T(8,128)(2,1)S(1)} %collective-permute-done.10.refs_1_) | copy-start | bytes 110596
  59.8 4.9 %collective-permute-start.11 = (bf16[2,72,128]{2,1,0:T(8,128)(2,1)S(1)}, bf16[2,72,128]{2,1,0:T(8,128)(2,1)S(1)}, u32[]{:S(2)}, u32[]{:S(2)}) collective-permute-start(bf16[2,72,128]{2,1,0:T(8,128)(2,1)S(1)} %pad_maximum_fusion.3), channel_id=1, source_target_pairs={{0,16},{8,24},{16,0},{24,8},{1,17},{9,25},{17,1},{25,9},{2,18},{10... | collective-permute-start | bytes 110600 | tf_op jit(solution)/shard_map/ppermute | solution.py:246
  64.6 6.3 %copy-start.9 = (bf16[2,72,128]{2,1,0:T(8,128)(2,1)}, bf16[2,72,128]{2,1,0:T(8,128)(2,1)S(1)}, u32[]{:S(2)}) copy-start(bf16[2,72,128]{2,1,0:T(8,128)(2,1)S(1)} %collective-permute-done.11.refs_2_) | copy-start | bytes 110596
  64.6 6.3 %collective-permute-start.12 = (bf16[2,72,128]{2,1,0:T(8,128)(2,1)S(1)}, bf16[2,72,128]{2,1,0:T(8,128)(2,1)S(1)}, u32[]{:S(2)}, u32[]{:S(2)}) collective-permute-start(bf16[2,72,128]{2,1,0:T(8,128)(2,1)S(1)} %pad_maximum_fusion.4), channel_id=1, source_target_pairs={{0,24},{8,16},{16,8},{24,0},{1,25},{9,17},{17,9},{25,1},{2,26},{10... | collective-permute-start | bytes 110600 | tf_op jit(solution)/shard_map/ppermute | solution.py:246
  71.0 0.6 copy-start.10
  73.1 0.8 copy-start
  73.9 0.8 copy-start.1
  108.1 2.2 %copy-start.11 = (f32[48,48]{1,0:T(8,128)S(1)}, f32[48,48]{1,0:T(8,128)}, u32[]{:S(2)}) copy-start(f32[48,48]{1,0:T(8,128)} %get-tuple-element.13) | copy-start | bytes 27652

commit v2 on v0

v2 whole, which is shorter than its diff:
```python
import functools
import math

import jax
import jax.numpy as jnp
from jax import lax
from jax.experimental import pallas as pl
from jax.experimental.pallas import tpu as pltpu
from jax.sharding import PartitionSpec as P

viscosity = 0.05
bf16 = jnp.bfloat16
f32 = jnp.float32
MIB = 2**20
CUTS = (0.5,)
TIED = 2

vmem = pl.BlockSpec(memory_space=pltpu.VMEM)
smem = pl.BlockSpec(memory_space=pltpu.SMEM)


def spread(rows):
    return pltpu.VMEM(rows, f32)


def room(*arrays):
    size = sum(math.prod(array.shape) * jnp.dtype(array.dtype).itemsize for array in arrays)
    spare = 4 * MIB if size < 24 * MIB else 24 * MIB
    return pltpu.CompilerParams(vmem_limit_bytes=int(min(60 * MIB, 1.2 * size + spare)))


def cost(microseconds):
    return pl.CostEstimate(
        flops=int(1e9 * microseconds), bytes_accessed=int(3e6 * microseconds), transcendentals=0
    )


def dot_last(left, right, **options):
    return lax.dot_general(
        left, right, (((1,), (1,)), ((), ())), preferred_element_type=f32, **options
    )


def head_kernel(sizes, me_ref, modes_ref, *refs):
    owners, spans = sizes
    *outs, turned = refs
    local, comps, planes, rows_y, cells = modes_ref.shape
    lanes = planes * rows_y
    per_cell = comps * local
    pieces = lanes // 128
    unit = (
        lax.broadcasted_iota(jnp.int32, (cells, cells), 0)
        == lax.broadcasted_iota(jnp.int32, (cells, cells), 1)
    ).astype(f32)
    unit = unit.astype(bf16)
    for comp in range(comps):
        for mode in range(local):
            field = modes_ref[mode, comp].reshape(lanes, cells)
            flipped = dot_last(unit, field)
            for piece in range(pieces):
                turned[piece, pl.ds(comp * local + mode, cells, stride=per_cell), :] = flipped[
                    :, piece * 128 : (piece + 1) * 128
                ]
    pairs = cells // 2 // owners
    for number, out in enumerate(outs):
        start, stop = spans[number // owners]
        target = me_ref[0] ^ (number % owners)
        for row in range(start, stop):
            pair = lax.rem(target * pairs + (row + cells // 2), cells // 2)
            first = pl.multiple_of(pair * (2 * per_cell), math.gcd(2 * per_cell, 8))
            for piece in range(pieces):
                out[row - start, :, piece * 128 : (piece + 1) * 128] = turned[
                    piece, pl.ds(first, 2 * per_cell), :
                ].astype(bf16)


def head(me, modes, owners, spans):
    local, comps, planes, rows_y, cells = modes.shape
    lanes = planes * rows_y
    height = 2 * comps * local
    shapes = [
        jax.ShapeDtypeStruct((stop - start, height, lanes), bf16)
        for start, stop in spans
        for unused in range(owners)
    ]
    turned = spread((lanes // 128, cells * comps * local, 128))
    results = pl.pallas_call(
        functools.partial(head_kernel, (owners, spans)),
        in_specs=[smem, vmem],
        out_specs=[vmem] * len(shapes),
        out_shape=shapes,
        scratch_shapes=[turned],
        compiler_params=room(modes, turned, *shapes),
        cost_estimate=cost(1.0),
        name="head",
    )(me, modes)
    return [results[q * owners : (q + 1) * owners] for q in range(len(spans))]


def pack_kernel(owners, planes, volume_ref, after_ref, out_ref):
    rows, cells = volume_ref.shape[1:]
    slabs = out_ref.shape[0] // owners
    depth = cells // owners
    by_slab = volume_ref[...].reshape(slabs, planes, rows, cells)
    for owner in range(owners):
        out_ref[owner * slabs : (owner + 1) * slabs, :] = jnp.concatenate(
            [
                by_slab[:, plane, row, owner * depth : (owner + 1) * depth]
                for plane in range(planes)
                for row in range(rows)
            ],
            axis=1,
        )


def pack(volume, after, owners, planes):
    devices = owners * (volume.shape[0] // planes)
    out_shape = jax.ShapeDtypeStruct((devices, volume.size // devices), f32)
    return pl.pallas_call(
        functools.partial(pack_kernel, owners, planes),
        in_specs=[vmem, pl.BlockSpec(memory_space=pl.ANY)],
        out_specs=vmem,
        out_shape=out_shape,
        compiler_params=room(volume, out_shape),
        cost_estimate=cost(0.3),
        name="pack",
    )(volume, after)


def assemble_kernel(edge, me_ref, *refs):
    *blocks, out_ref, edge_ref, wide = refs
    local = blocks[0].shape[1] // 6
    total = local * len(blocks)
    rows = blocks[0].shape[0]
    place = 0
    for row in range(rows):
        for shift, block in enumerate(blocks):
            first = (me_ref[0] ^ shift) * local
            values = block[row].astype(f32)
            for part in range(6):
                for piece in range(wide.shape[1]):
                    wide[row, piece, pl.ds(part * total + first, local), :] = values[
                        part * local : (part + 1) * local, piece * 128 : (piece + 1) * 128
                    ]
    for row in range(rows):
        for piece in range(wide.shape[1]):
            lanes = slice(piece * 128, (piece + 1) * 128)
            merged = wide[row, piece].astype(bf16)
            if row == edge:
                edge_ref[0, :, lanes] = merged
            else:
                out_ref[place, :, lanes] = merged
        place += row != edge


def assemble(me, blocks, edge):
    rows, height, lanes = blocks[0].shape
    height *= len(blocks)
    body = rows - (edge is not None)
    wide = spread((rows, lanes // 128, height, 128))
    out_shape = (
        jax.ShapeDtypeStruct((body, height, lanes), bf16),
        jax.ShapeDtypeStruct((1, height, lanes), bf16),
    )
    return pl.pallas_call(
        functools.partial(assemble_kernel, edge),
        in_specs=[smem] + [vmem] * len(blocks),
        out_specs=(vmem, vmem),
        out_shape=out_shape,
        scratch_shapes=[wide],
        compiler_params=room(wide, *blocks, *out_shape),
        cost_estimate=cost(0.2),
        name="assemble",
    )(me, *blocks)


def central(first, second, fourth, fifth):
    return ((first - fifth) * (1.0 / 12.0) + (fourth - second) * (8.0 / 12.0)).astype(bf16)


def repack(ref, out, groups):
    rows = [ref[pl.ds(number, groups, stride=8), :][:, :48] for number in range(8)]
    out[pl.ds(0, groups, stride=3), :] = jnp.concatenate(
        [rows[0], rows[1], rows[2][:, :32]], axis=1
    )
    out[pl.ds(1, groups, stride=3), :] = jnp.concatenate(
        [rows[2][:, 32:], rows[3], rows[4], rows[5][:, :16]], axis=1
    )
    out[pl.ds(2, groups, stride=3), :] = jnp.concatenate(
        [rows[5][:, 16:], rows[6], rows[7]], axis=1
    )


def unpack(ref, first, groups):
    wide = [ref[pl.ds(first + number, groups, stride=3), :] for number in range(3)]
    return [
        wide[0][:, :48],
        wide[0][:, 48:96],
        jnp.concatenate([wide[0][:, 96:], wide[1][:, :16]], axis=1),
        wide[1][:, 16:64],
        wide[1][:, 64:112],
        jnp.concatenate([wide[1][:, 112:], wide[2][:, :32]], axis=1),
        wide[2][:, 32:80],
        wide[2][:, 80:],
    ]


def galerkin_kernel(field_plan, halo_plan, has_sum, packs, rows_y, depth, core_ref, *refs):
    count = len(halo_plan)
    refs = list(refs)
    conv_in, diss_in = (refs.pop(0), refs.pop(0)) if has_sum else (None, None)
    volume_ref = refs.pop(0)
    if refs[-2].shape != refs[-1].shape:
        refs.append(refs[-1])
    fields, low, high, weights_ref, carried0, carried1 = refs[-6:]
    buffers = (refs[-14:-10], refs[-10:-6])
    if packs:
        flat, packed_diss, diss_ref, conv_ref = refs[-18:-14]
        message_ref = refs[-19]
        sources = refs[:-19]
    else:
        conv_ref, diss_ref = refs[-16:-14]
        sources = refs[:-16]
    height, lanes = fields.shape[1:]
    half = height // 2
    mode_count = half // 3
    width = 2 * lanes

    for slot, (operand, row) in enumerate(field_plan):
        fields[slot] = sources[operand][row]
    odd_core = core_ref[0] == 1

    def fill(lower, upper):
        for slot, (inter, intra, row, unused) in enumerate(halo_plan):
            lower[slot] = sources[inter][row]
            upper[slot] = sources[intra][row]

    @pl.when(odd_core)
    def odd():
        fill(high, low)

    @pl.when(jnp.logical_not(odd_core))
    def even():
        fill(low, high)

    if has_sum:
        conv_ref[...] = conv_in[...]
        diss_ref[...] = diss_in[...]
    else:
        conv_ref[...] = jnp.zeros_like(conv_ref)
        diss_ref[...] = jnp.zeros_like(diss_ref)

    devices = volume_ref.shape[0]
    rows = rows_y // devices
    lane = lax.broadcasted_iota(jnp.int32, (devices, lanes), 1)
    device = lax.broadcasted_iota(jnp.int32, (devices, lanes), 0)
    weights = jnp.zeros((depth, lanes), f32)
    for plane in range(lanes // rows_y):
        for row in range(rows):
            place = (plane * rows + row) * depth
            chosen = (lane == plane * rows_y + device * rows + row).astype(f32)
            weights += lax.dot_general(
                volume_ref[:, place : place + depth],
                chosen,
                (((0,), (0,)), ((), ())),
                preferred_element_type=f32,
                precision=lax.Precision.HIGHEST,
            )
    weights_ref[...] = weights
    for buffer in buffers:
        buffer[3][2 * mode_count :, :] = jnp.zeros_like(buffer[3][2 * mode_count :, :])
        buffer[1][mode_count:, :] = jnp.zeros_like(buffer[1][mode_count:, :])

    row_y = lax.broadcasted_iota(jnp.int32, (height, lanes), 1) % rows_y

    def shifted(array, step):
        moved = pltpu.roll(array, (-step) % lanes, 1)
        inside = (row_y + step >= 0) & (row_y + step < rows_y)
        return jnp.where(inside, moved, 0.0)

    first_cell = halo_plan[0][3]

    def gradients(step, buffer):
        slopes, scaled, values, stationary = buffer
        before = fields[step].astype(f32)
        here = fields[step + 1].astype(f32)
        after = fields[step + 2].astype(f32)
        left = low[step].astype(f32)
        right = high[step].astype(f32)
        along_x = central(
            left,
            jnp.concatenate([left[:, rows_y:], here[:, : lanes - rows_y]], axis=1),
            jnp.concatenate([here[:, rows_y:], right[:, : lanes - rows_y]], axis=1),
            right,
        )
        along_y = central(shifted(here, -2), shifted(here, -1), shifted(here, 1), shifted(here, 2))
        along_z = jnp.concatenate(
            [
                central(before[:half], before[half:], here[half:], after[:half]),
                central(before[half:], here[:half], after[:half], after[half:]),
            ],
            axis=0,
        )
        for parity in range(2):
            span = slice(parity * lanes, (parity + 1) * lanes)
            own = slice(parity * half, (parity + 1) * half)
            weights = weights_ref[pl.ds(2 * (first_cell + step) + parity, 1), :]
            values[:, span] = fields[step + 1, own, :]
            product = here[own] * weights
            coarse = product.astype(bf16)
            fine = (product - coarse.astype(f32)).astype(bf16)
            for comp in range(3):
                modes = slice(comp * mode_count, (comp + 1) * mode_count)
                place = slice((2 * comp + parity) * lanes, (2 * comp + parity + 1) * lanes)
                stationary[:mode_count, place] = coarse[modes]
                stationary[mode_count : 2 * mode_count, place] = fine[modes]
                for direction, along in enumerate((along_x, along_y, along_z)):
                    number = comp * 3 + direction
                    begin = parity * half + comp * mode_count
                    piece = along[begin : begin + mode_count]
                    slopes[number * mode_count : (number + 1) * mode_count, span] = piece
                    begin = number * width + parity * lanes
                    scaled[:mode_count, begin : begin + lanes] = (piece.astype(f32) * weights).astype(bf16)

    def contract(buffer, carried):
        slopes, scaled, values, stationary = buffer
        side = jnp.concatenate(
            [slopes[number * mode_count : (number + 1) * mode_count, :] for number in range(9)],
            axis=1,
        )
        diss_ref[...] += dot_last(side, scaled[...])
        for j in range(mode_count):
            rows = [
                jnp.broadcast_to(
                    values[b * mode_count + j : b * mode_count + j + 1, :], (mode_count, width)
                )
                for b in range(3)
            ]
            for a in range(3):
                parts = [
                    slopes[(a * 3 + b) * mode_count : (a * 3 + b + 1) * mode_count, :]
                    for b in range(3)
                ]
                carried[j * mode_count : (j + 1) * mode_count, a * width : (a + 1) * width] = (
                    rows[0] * parts[0] + rows[1] * parts[1] + rows[2] * parts[2]
                )
        conv_ref[...] += dot_last(carried[...], stationary[...])

    gradients(0, buffers[0])

    def two_steps(number, unused):
        gradients(2 * number + 1, buffers[1])
        contract(buffers[0], carried0)
        gradients(jnp.minimum(2 * number + 2, count - 1), buffers[0])
        contract(buffers[1], carried1)
        return unused

    lax.fori_loop(0, count // 2, two_steps, 0)
    if count % 2:
        contract(buffers[0], carried0)

    if packs:
        chunks = mode_count * mode_count // 128
        for chunk in range(chunks):
            part = conv_ref[chunk * 128 : (chunk + 1) * 128, :].T
            flat[pl.ds(chunk, mode_count, stride=chunks), :] = (
                part[:mode_count] + part[mode_count : 2 * mode_count]
            )
        repack(diss_ref, packed_diss, mode_count // 8)
        devices, total, unused = message_ref.shape
        share = total - packed_diss.shape[0]
        tail = packed_diss[...]
        for device in range(devices):
            message_ref[device] = jnp.concatenate(
                [flat[device * share : (device + 1) * share, :], tail], axis=0
            ).astype(bf16)


def galerkin(core, sums, volume, sources, field_plan, halo_plan, rows_y, depth, message):
    height, lanes = sources[0].shape[1:]
    mode_count = height // 6
    used = sorted({e[0] for e in field_plan} | {o for e in halo_plan for o in e[:2]})
    number = {operand: place for place, operand in enumerate(used)}
    field_plan = tuple((number[operand], row) for operand, row in field_plan)
    halo_plan = tuple((number[p], number[q], row, cell) for p, q, row, cell in halo_plan)
    operands = list(sums or ()) + [volume] + [sources[operand] for operand in used]
    square = mode_count * mode_count
    scratch = []
    if message is None:
        out_shape = (
            jax.ShapeDtypeStruct((square, 128), f32),
            jax.ShapeDtypeStruct((mode_count, 128), f32),
        )
    else:
        out_shape = jax.ShapeDtypeStruct(message, bf16)
        scratch = [
            pltpu.VMEM((mode_count * square // 128, 128), f32),
            pltpu.VMEM((square // 128, 128), f32),
            pltpu.VMEM((mode_count, 128), f32),
            pltpu.VMEM((square, 128), f32),
        ]
    buffers = [
        pltpu.VMEM((9 * mode_count, 2 * lanes), bf16),
        pltpu.VMEM((128, 18 * lanes), bf16),
        pltpu.VMEM((3 * mode_count, 2 * lanes), bf16),
        pltpu.VMEM((128, 6 * lanes), bf16),
    ]
    scratch += (
        buffers
        + buffers
        + [
            pltpu.VMEM((len(field_plan), height, lanes), bf16),
            pltpu.VMEM((len(halo_plan), height, lanes), bf16),
            pltpu.VMEM((len(halo_plan), height, lanes), bf16),
            pltpu.VMEM((depth, lanes), f32),
        ]
        + [pltpu.VMEM((square, 6 * lanes), bf16)] * (2 if lanes <= 128 else 1)
    )
    shapes = out_shape if message is None else (out_shape,)
    return pl.pallas_call(
        functools.partial(
            galerkin_kernel, field_plan, halo_plan, sums is not None, message is not None, rows_y,
            depth,
        ),
        in_specs=[smem] + [vmem] * len(operands),
        out_specs=vmem if message is not None else (vmem, vmem),
        out_shape=out_shape,
        scratch_shapes=scratch,
        compiler_params=room(*operands, *shapes, *scratch),
        cost_estimate=cost(1.4 * len(halo_plan) + 0.5),
        name="galerkin",
    )(core, *operands)


def finish_kernel(scales, moved_ref, conv_ref, diss_ref, total):
    total[...] = jnp.sum(moved_ref[...].astype(f32), axis=0)
    groups = conv_ref.shape[0] // 8
    for number, rows in enumerate(unpack(total, 0, groups)):
        conv_ref[pl.ds(number, groups, stride=8), :] = rows * scales[0]
    first = 3 * groups
    groups = diss_ref.shape[0] // 8
    for number, rows in enumerate(unpack(total, first, groups)):
        diss_ref[pl.ds(number, groups, stride=8), :] = rows * scales[1]


def finish(moved, mode_count, scales):
    devices = moved.shape[0]
    return pl.pallas_call(
        functools.partial(finish_kernel, scales),
        in_specs=[vmem],
        out_specs=(vmem, vmem),
        out_shape=(
            jax.ShapeDtypeStruct((mode_count * mode_count // devices, mode_count), f32),
            jax.ShapeDtypeStruct((mode_count, mode_count), f32),
        ),
        scratch_shapes=[pltpu.VMEM(moved.shape[1:], f32)],
        compiler_params=room(moved, jax.ShapeDtypeStruct(moved.shape, f32)),
        cost_estimate=cost(0.8),
        name="finish",
    )(moved)


def per_device(modes, volume):
    local, comps, planes, rows_y, cells = modes.shape
    owners = lax.axis_size("mode")
    slabs = lax.axis_size("slab")
    devices = owners * slabs
    mode_count = local * owners
    lanes = planes * rows_y
    pairs = cells // 2 // owners
    me = lax.axis_index("mode").astype(jnp.int32).reshape(1)
    position = (lax.axis_index("slab") % 2).astype(jnp.int32).reshape(1)

    cuts = [0] + [int(pairs * cut) for cut in CUTS] + [pairs]
    chunks = len(cuts) - 1
    spans = tuple(
        (cuts[q] - (q == 0), cuts[q + 1] + (q == chunks - 1)) for q in range(chunks)
    )
    messages = head(me, modes, owners, spans)

    weights = pack(volume, messages[0][0], owners, planes)
    weights = lax.all_to_all(weights, ("mode", "slab"), 0, 0, tiled=True)

    def exchange(blocks):
        moved = [blocks[0]]
        for shift in range(1, owners):
            moved.append(
                lax.ppermute(
                    blocks[shift], "mode", [(source, source ^ shift) for source in range(owners)]
                )
            )
        return moved

    inter = [(i, i + 1) for i in range(1, slabs - 1, 2)]
    inter += [(j, i) for i, j in inter]
    intra = [(i, i ^ 1) for i in range(slabs)]

    sources = []
    for q in range(chunks):
        edge = 0 if q == 0 else (spans[q][1] - spans[q][0] - 1 if q == chunks - 1 else None)
        blocks = exchange(messages[q])
        body, edge_row = assemble(me, blocks, edge)
        between = lax.ppermute(body, "slab", inter)
        within = lax.ppermute(body, "slab", intra)
        sources += [body, edge_row, between, within]
        if q + 1 < chunks:
            tied = TIED
            *held, messages[q + 1] = lax.optimization_barrier((*blocks[1 : 1 + tied], messages[q + 1]))

    def place(row):
        if row < 0:
            return (1, 0)
        if row >= pairs:
            return (4 * chunks - 3, 0)
        q = max(q for q in range(chunks) if cuts[q] <= row)
        return (4 * q, row - cuts[q])

    sums = None
    share = mode_count**3 // devices
    fast = share % 384 == 0 and mode_count == 48
    message = (devices, (share + mode_count**2) // 128, 128) if fast else None
    for q in range(chunks):
        last = q == chunks - 1
        start = cuts[q] - (q > 0)
        stop = pairs if last else cuts[q + 1] - 1
        field_plan = [place(row) for row in range(start - 1, stop + 1)]
        halo_plan = []
        for row in range(start, stop):
            operand, inner = place(row)
            halo_plan.append((operand + 2, operand + 3, inner, row))
        sums = galerkin(
            position, sums, weights, sources, field_plan, halo_plan, rows_y,
            cells // owners, message if last else None,
        )

    total_cells = cells * rows_y * planes * slabs
    scales = (1.0 / math.sqrt(total_cells), viscosity / total_cells)
    if fast:
        moved = lax.all_to_all(sums, ("mode", "slab"), 0, 0, tiled=True)
        return finish(moved, mode_count, scales)
    conv, diss = sums
    conv = conv[:, :mode_count] + conv[:, mode_count : 2 * mode_count]
    padded = -(-share // 128) * 128
    conv = conv.T.reshape(devices, share)
    conv = jnp.pad(conv, ((0, 0), (0, padded - share))).reshape(devices, padded // 128, 128)
    extra = jnp.broadcast_to(
        diss[:, :mode_count].reshape(1, -1, 128), (devices, mode_count**2 // 128, 128)
    )
    packed = jnp.concatenate([conv, extra], axis=1).astype(bf16)
    moved = lax.all_to_all(packed, ("mode", "slab"), 0, 0, tiled=True).astype(f32).sum(0)
    convective = moved[: padded // 128].reshape(padded)[:share].reshape(-1, mode_count)
    dissipation = moved[padded // 128 :].reshape(mode_count, mode_count)
    return (convective * scales[0], dissipation * scales[1])


def solution(mesh):
    placed = (P("mode", None, "slab", None, None), P(None, ("mode", "slab"), None))
    return jax.shard_map(
        per_device,
        mesh=mesh,
        in_specs=placed,
        out_specs=(P(("mode", "slab"), None), P()),
        check_vma=False,
    )
```

time: 562 us -> 94.5 us (0.17)
  blocking collectives: 144 us -> 22.1 us
  local copies, waits for them, and re-layouts: 114 us -> 3.46 us
  other arithmetic: 94.4 us -> 0 us
  waiting for transfers between devices: 110 us -> 18.8 us
  matrix products: 48.7 us -> 0 us
  Pallas kernels: 0 us -> 26.1 us
  between operations: 14.2 us -> 0.79 us
  starting transfers between devices: 35.6 us -> 23 us
    convert_element_type x8 -> x0, other arithmetic: 85 us -> none  [the longest x4 79.5 us: one_step(): carried = (carried * piece_weights).astype(jnp.bfloat16).reshape(mode_cou...]
    all_to_all x1, blocking collectives: 105 us -> 22.1 us  [per_device(): moved = lax.all_to_all(sums, ('mode', 'slab'), 0, 0, tiled=True)]
    unnamed x2 -> x0, waiting for transfers between devices: 55.2 us -> none
    all_to_all x1, waiting for transfers between devices: 54.8 us -> 3.13 us  [per_device(): weights = lax.all_to_all(weights, ('mode', 'slab'), 0, 0, tiled=True)]
    dot_general x8 -> x0, matrix products: 48.7 us -> none  [the longest x4 41 us: one_step(): lax.dot_general(piece_values.reshape(mode_count, 3 * block_size), carried...]
    while x32 -> x0, local copies, waits for them, and re-layouts: 45 us -> none
    psum x1 -> x0, blocking collectives: 38.1 us -> none  [per_device(): diss_sum = lax.psum(diss_part, ('mode', 'slab'))]
    pallas_call x0 -> x7, Pallas kernels: none -> 26.1 us  [the longest x2 23.2 us: galerkin(): pl.pallas_call(functools.partial(galerkin_kernel, field_plan, halo_plan,...]
  transfers between devices with their start and end apart: 4 -> 11, of which waited for: 3 -> 4; matrix products, arithmetic and copies ran while one was open for 1% -> 0% of each run, Pallas kernels for 0% -> 12%
where the time goes in v2:
time: 94.5 us; the launch traced here: 94.2 us
  Pallas kernels  26.1 us (28%)
  starting transfers between devices  23 us (24%)
  blocking collectives  22.1 us (23%)
  waiting for transfers between devices  18.8 us (20%)
  local copies, waits for them, and re-layouts  3.46 us (4%)
    pallas_call x2, Pallas kernels, galerkin(): pl.pallas_call(functools.partial(galerkin_kernel, field_plan, halo_plan,...  23.2 us
    all_to_all x1, blocking collectives, per_device(): moved = lax.all_to_all(sums, ('mode', 'slab'), 0, 0, tiled=True)  22.1 us
    ppermute x6, waiting for transfers between devices, exchange(): lax.ppermute(blocks[shift], 'mode', [(source, source ^ shift) for source...  15.6 us
    ppermute x6, starting transfers between devices, exchange(): lax.ppermute(blocks[shift], 'mode', [(source, source ^ shift) for source...  10.9 us
    all_to_all x1, starting transfers between devices, per_device(): weights = lax.all_to_all(weights, ('mode', 'slab'), 0, 0, tiled=True)  6.52 us
    ppermute x2, starting transfers between devices, per_device(): within = lax.ppermute(body, 'slab', intra)  4.22 us
    all_to_all x1, waiting for transfers between devices, per_device(): weights = lax.all_to_all(weights, ('mode', 'slab'), 0, 0, tiled=True)  3.13 us
    unnamed x12, local copies, waits for them, and re-layouts  2.77 us
  transfers between devices with their start and end apart: 11, of which 4 were waited for; matrix products, arithmetic and copies ran while one was open for 0% of the time, Pallas kernels for 12%

profile of v2, /device:TPU:0, one launch (start us, length us, event | category | flops | bytes accessed | tf_op | source)
XLA Modules:
  0.0 94.2 jit_solution(17237955572785346828)
XLA Ops:
  0.6 0.0 copy-start
  0.6 1.3 %copy-done = bf16[12,3,2,64,128]{4,3,2,1,0:T(8,128)(2,1)S(1)} copy-done((bf16[12,3,2,64,128]{4,3,2,1,0:T(8,128)(2,1)S(1)}, bf16[12,3,2,64,128]{4,3,2,1,0:T(8,128)(2,1)}, u32[]{:S(2)}) %copy-start) | copy-done | bytes 1179672
  1.9 0.0 copy-start.1
  1.9 1.1 %head.1 = (bf16[9,72,128]{2,1,0:T(8,128)(2,1)S(1)}, bf16[9,72,128]{2,1,0:T(8,128)(2,1)S(1)}, bf16[9,72,128]{2,1,0:T(8,128)(2,1)S(1)}, bf16[9,72,128]{2,1,0:T(8,1...) custom-call(s32[1]{0:T(128)} %bitcast.1.me_ref, ...), custom_call_target="tpu_custom_call" | custom-call | flops 1000000000 | bytes 3000000 | tf_op jit(solution)/shard_map/head/pallas_call | solution.py:87
  3.0 3.1 %collective-permute-start = (bf16[9,72,128]{2,1,0:T(8,128)(2,1)S(1)}, bf16[9,72,128]{2,1,0:T(8,128)(2,1)S(1)}, u32[]{:S(2)}, u32[]{:S(2)}) collective-permute-start(bf16[9,72,128]{2,1,0:T(8,128)(2,1)S(1)} %get-tuple-element.21), channel_id=1, source_target_pairs={{0,8},{8,0},{16,24},{24,16},{1,9},{9,1},{17,25},{25,17},{2,10},{10... | collective-permute-start | bytes 497672 | tf_op jit(solution)/shard_map/ppermute | solution.py:488
  6.1 2.6 %collective-permute-start.1 = (bf16[9,72,128]{2,1,0:T(8,128)(2,1)S(1)}, bf16[9,72,128]{2,1,0:T(8,128)(2,1)S(1)}, u32[]{:S(2)}, u32[]{:S(2)}) collective-permute-start(bf16[9,72,128]{2,1,0:T(8,128)(2,1)S(1)} %get-tuple-element.22), channel_id=1, source_target_pairs={{0,16},{8,24},{16,0},{24,8},{1,17},{9,25},{17,1},{25,9},{2,18},{10... | collective-permute-start | bytes 497672 | tf_op jit(solution)/shard_map/ppermute | solution.py:488
  8.7 0.0 collective-permute-start.2
  8.7 4.2 %collective-permute-done.refs_1_ = bf16[9,72,128]{2,1,0:T(8,128)(2,1)S(1)} collective-permute-done((bf16[9,72,128]{2,1,0:T(8,128)(2,1)S(1)}, bf16[9,72,128]{2,1,0:T(8,128)(2,1)S(1)}, u32[]{:S(2)}, u32[]{:S(2)}) %collective-permute-start) | collective-permute-done | bytes 165920 | tf_op jit(solution)/shard_map/ppermute | solution.py:488
  12.9 8.4 %collective-permute-done.1.refs_2_ = bf16[9,72,128]{2,1,0:T(8,128)(2,1)S(1)} collective-permute-done((bf16[9,72,128]{2,1,0:T(8,128)(2,1)S(1)}, bf16[9,72,128]{2,1,0:T(8,128)(2,1)S(1)}, u32[]{:S(2)}, u32[]{:S(2)}) %collective-permute-start.1) | collective-permute-done | bytes 165920 | tf_op jit(solution)/shard_map/ppermute | solution.py:488
  21.3 0.0 collective-permute-done.2.refs_3_
  21.3 0.2 assemble.2
  21.4 0.0 copy-start.2
  21.4 0.1 collective-permute-start.4
  21.5 0.7 collective-permute-start.3
  22.2 2.8 %collective-permute-start.5 = (bf16[9,72,128]{2,1,0:T(8,128)(2,1)S(1)}, bf16[9,72,128]{2,1,0:T(8,128)(2,1)S(1)}, u32[]{:S(2)}, u32[]{:S(2)}) collective-permute-start(bf16[9,72,128]{2,1,0:T(8,128)(2,1)S(1)} %get-tuple-element.33), channel_id=1, source_target_pairs={{0,8},{8,0},{16,24},{24,16},{1,9},{9,1},{17,25},{25,17},{2,10},{10... | collective-permute-start | bytes 497672 | tf_op jit(solution)/shard_map/ppermute | solution.py:488
  25.0 1.1 %collective-permute-start.6 = (bf16[9,72,128]{2,1,0:T(8,128)(2,1)S(1)}, bf16[9,72,128]{2,1,0:T(8,128)(2,1)S(1)}, u32[]{:S(2)}, u32[]{:S(2)}) collective-permute-start(bf16[9,72,128]{2,1,0:T(8,128)(2,1)S(1)} %get-tuple-element.34), channel_id=1, source_target_pairs={{0,16},{8,24},{16,0},{24,8},{1,17},{9,25},{17,1},{25,9},{2,18},{10... | collective-permute-start | bytes 497672 | tf_op jit(solution)/shard_map/ppermute | solution.py:488
  26.1 1.4 %collective-permute-start.7 = (bf16[9,72,128]{2,1,0:T(8,128)(2,1)S(1)}, bf16[9,72,128]{2,1,0:T(8,128)(2,1)S(1)}, u32[]{:S(2)}, u32[]{:S(2)}) collective-permute-start(bf16[9,72,128]{2,1,0:T(8,128)(2,1)S(1)} %get-tuple-element.35), channel_id=1, source_target_pairs={{0,24},{8,16},{16,8},{24,0},{1,25},{9,17},{17,9},{25,1},{2,26},{10... | collective-permute-start | bytes 497672 | tf_op jit(solution)/shard_map/ppermute | solution.py:488
  27.5 0.0 copy-done.1
  27.5 0.7 pack.1
  28.1 0.0 copy-done.2
  28.2 6.5 %all-to-all-start = ((f32[32,1,128]{2,1,0:T(1,128)}), f32[32,1,128]{2,1,0:T(1,128)S(1)}, u32[]{:S(2)}, u32[]{:S(2)}) async-start(f32[32,1,128]{2,1,0:T(1,128)} %bitcast.3), calls=%async_computation | async-start | bytes 32768 | tf_op jit(solution)/shard_map/all_to_all | solution.py:482
  34.7 0.0 collective-permute-done.5.refs_1_
  34.7 0.0 collective-permute-done.6.refs_2_
  34.7 3.0 %collective-permute-done.7.refs_3_ = bf16[9,72,128]{2,1,0:T(8,128)(2,1)S(1)} collective-permute-done((bf16[9,72,128]{2,1,0:T(8,128)(2,1)S(1)}, bf16[9,72,128]{2,1,0:T(8,128)(2,1)S(1)}, u32[]{:S(2)}, u32[]{:S(2)}) %collective-permute-start.7) | collective-permute-done | bytes 165920 | tf_op jit(solution)/shard_map/ppermute | solution.py:488
  37.7 0.2 assemble.3
  37.9 0.0 copy-start.4
  37.9 0.6 copy-done.4
  38.5 4.1 %collective-permute-start.9 = (bf16[8,288,128]{2,1,0:T(8,128)(2,1)S(1)}, bf16[8,288,128]{2,1,0:T(8,128)(2,1)S(1)}, u32[]{:S(2)}, u32[]{:S(2)}) collective-permute-start(bf16[8,288,128]{2,1,0:T(8,128)(2,1)S(1)} %get-tuple-element.36.refs_6_), channel_id=1, source_target_pairs={{0,1},{1,0},{2,3},{3,2},{4,5},{5,4},{6,7},{7,6},{8,9},{9,8},{10,11... | collective-permute-start | bytes 1769480 | tf_op jit(solution)/shard_map/ppermute | solution.py:504
  42.7 0.7 collective-permute-start.8
  43.4 3.1 %all-to-all-done = f32[32,1,128]{2,1,0:T(1,128)S(1)} async-done(((f32[32,1,128]{2,1,0:T(1,128)}), f32[32,1,128]{2,1,0:T(1,128)S(1)}, u32[]{:S(2)}, u32[]{:S(2)}) %all-to-all-start) | async-done | bytes 16416 | tf_op jit(solution)/shard_map/all_to_all | solution.py:482
  46.5 0.0 collective-permute-done.4.refs_4_.refs_5_
  46.5 0.0 collective-permute-done.3.refs_3_.refs_4_
  46.5 0.0 copy-start.3
  46.5 0.9 copy-done.3
  47.4 0.0 copy-start.5
  47.4 10.2 %galerkin.2 = (f32[2304,128]{1,0:T(8,128)S(1)}, f32[48,128]{1,0:T(8,128)S(1)}) custom-call(s32[1]{0:T(128)} %bitcast.core_ref, f32[32,128]{1,0:T(8,128)S(1)} %bitcast.6, bf16[8,288,128]{2,1,0:T(8,128)(2,1)S(1)} %get-tuple-element.24.refs_1_.refs_3_, bf16[1,288,128]{2,1,0:T(8,128)(2,1)S(1)} %copy-done.3, ...), custom_call_target="tpu_custom_call" | custom-call | flops 10300000256 | bytes 30900000 | tf_op jit(solution)/shard_map/galerkin/pallas_call | solution.py:420
  57.6 0.0 collective-permute-done.9.refs_9_
  57.6 0.0 collective-permute-done.8.refs_8_
  57.6 0.0 copy-done.5
  57.6 13.0 %galerkin.3 = bf16[32,45,128]{2,1,0:T(8,128)(2,1)S(1)} custom-call(s32[1]{0:T(128)} %bitcast.core_ref, f32[2304,128]{1,0:T(8,128)S(1)} %get-tuple-element.26.refs_0_, f32[48,128]{1,0:T(8,128)S(1)} %get-tuple-element.27.refs_1_, f32[32,128]{1,0:T(8,128)S(1)} %bitcast.7, bf16[8,288,128]{2,1,0:T(8,128)(2,1)S(1)} %get-tuple-element.24.refs_1_.refs_3_, ...), custom_call_target="tpu_custom_call" | custom-call | flops 13100000256 | bytes 39300000 | tf_op jit(solution)/shard_map/galerkin/pallas_call | solution.py:420
  70.6 22.1 %all_to_all.16.moved_ref = bf16[32,45,128]{2,1,0:T(8,128)(2,1)S(1)} all-to-all(bf16[32,45,128]{2,1,0:T(8,128)(2,1)S(1)} %galerkin.3), channel_id=1, replica_groups=mesh['mode'=4,'slab'=8] {'mode','slab'}, dimensions={0} | all-to-all | bytes 737280 | tf_op jit(solution)/shard_map/all_to_all | solution.py:539
  92.7 0.8 finish.1
  93.5 0.7 copy.6
Async XLA Ops:
  0.6 1.3 %copy-start = (bf16[12,3,2,64,128]{4,3,2,1,0:T(8,128)(2,1)S(1)}, bf16[12,3,2,64,128]{4,3,2,1,0:T(8,128)(2,1)}, u32[]{:S(2)}) copy-start(bf16[12,3,2,64,128]{4,3,2,1,0:T(8,128)(2,1)} %modes_ref.1) | copy-start | bytes 3538948
  1.9 25.6 %copy-start.1 = (f32[16,2,128]{2,1,0:T(2,128)S(1)}, f32[16,2,128]{2,1,0:T(2,128)}, u32[]{:S(2)}) copy-start(f32[16,2,128]{2,1,0:T(2,128)} %volume_ref.1) | copy-start | bytes 49156
  3.0 9.9 %collective-permute-start = (bf16[9,72,128]{2,1,0:T(8,128)(2,1)S(1)}, bf16[9,72,128]{2,1,0:T(8,128)(2,1)S(1)}, u32[]{:S(2)}, u32[]{:S(2)}) collective-permute-start(bf16[9,72,128]{2,1,0:T(8,128)(2,1)S(1)} %get-tuple-element.21), channel_id=1, source_target_pairs={{0,8},{8,0},{16,24},{24,16},{1,9},{9,1},{17,25},{25,17},{2,10},{10... | collective-permute-start | bytes 497672 | tf_op jit(solution)/shard_map/ppermute | solution.py:488
  6.1 15.2 %collective-permute-start.1 = (bf16[9,72,128]{2,1,0:T(8,128)(2,1)S(1)}, bf16[9,72,128]{2,1,0:T(8,128)(2,1)S(1)}, u32[]{:S(2)}, u32[]{:S(2)}) collective-permute-start(bf16[9,72,128]{2,1,0:T(8,128)(2,1)S(1)} %get-tuple-element.22), channel_id=1, source_target_pairs={{0,16},{8,24},{16,0},{24,8},{1,17},{9,25},{17,1},{25,9},{2,18},{10... | collective-permute-start | bytes 497672 | tf_op jit(solution)/shard_map/ppermute | solution.py:488
  8.7 12.6 %collective-permute-start.2 = (bf16[9,72,128]{2,1,0:T(8,128)(2,1)S(1)}, bf16[9,72,128]{2,1,0:T(8,128)(2,1)S(1)}, u32[]{:S(2)}, u32[]{:S(2)}) collective-permute-start(bf16[9,72,128]{2,1,0:T(8,128)(2,1)S(1)} %get-tuple-element.23), channel_id=1, source_target_pairs={{0,24},{8,16},{16,8},{24,0},{1,25},{9,17},{17,9},{25,1},{2,26},{10... | collective-permute-start | bytes 497672 | tf_op jit(solution)/shard_map/ppermute | solution.py:488
  21.4 6.7 %copy-start.2 = (bf16[1,288,128]{2,1,0:T(8,128)(2,1)}, bf16[1,288,128]{2,1,0:T(8,128)(2,1)S(1)}, u32[]{:S(2)}) copy-start(bf16[1,288,128]{2,1,0:T(8,128)(2,1)S(1)} %get-tuple-element.25.refs_2_) | copy-start | bytes 221188
  21.4 25.1 %collective-permute-start.4 = (bf16[8,288,128]{2,1,0:T(8,128)(2,1)S(1)}, bf16[8,288,128]{2,1,0:T(8,128)(2,1)S(1)}, u32[]{:S(2)}, u32[]{:S(2)}) collective-permute-start(bf16[8,288,128]{2,1,0:T(8,128)(2,1)S(1)} %get-tuple-element.24.refs_1_.refs_3_), channel_id=1, source_target_pairs={{0,1},{1,0},{2,3},{3,2},{4,5},{5,4},{6,7},{7,6},{8,9},{9,8},{10,11... | collective-permute-start | bytes 1769480 | tf_op jit(solution)/shard_map/ppermute | solution.py:504
  21.5 25.0 %collective-permute-start.3 = (bf16[8,288,128]{2,1,0:T(8,128)(2,1)S(1)}, bf16[8,288,128]{2,1,0:T(8,128)(2,1)S(1)}, u32[]{:S(2)}, u32[]{:S(2)}) collective-permute-start(bf16[8,288,128]{2,1,0:T(8,128)(2,1)S(1)} %get-tuple-element.24.refs_1_.refs_3_), channel_id=1, source_target_pairs={{1,2},{3,4},{5,6},{2,1},{4,3},{6,5},{9,10},{11,12},{13,14},{10,9},... | collective-permute-start | bytes 1769480 | tf_op jit(solution)/shard_map/ppermute | solution.py:503
  22.2 12.5 %collective-permute-start.5 = (bf16[9,72,128]{2,1,0:T(8,128)(2,1)S(1)}, bf16[9,72,128]{2,1,0:T(8,128)(2,1)S(1)}, u32[]{:S(2)}, u32[]{:S(2)}) collective-permute-start(bf16[9,72,128]{2,1,0:T(8,128)(2,1)S(1)} %get-tuple-element.33), channel_id=1, source_target_pairs={{0,8},{8,0},{16,24},{24,16},{1,9},{9,1},{17,25},{25,17},{2,10},{10... | collective-permute-start | bytes 497672 | tf_op jit(solution)/shard_map/ppermute | solution.py:488
  25.0 9.7 %collective-permute-start.6 = (bf16[9,72,128]{2,1,0:T(8,128)(2,1)S(1)}, bf16[9,72,128]{2,1,0:T(8,128)(2,1)S(1)}, u32[]{:S(2)}, u32[]{:S(2)}) collective-permute-start(bf16[9,72,128]{2,1,0:T(8,128)(2,1)S(1)} %get-tuple-element.34), channel_id=1, source_target_pairs={{0,16},{8,24},{16,0},{24,8},{1,17},{9,25},{17,1},{25,9},{2,18},{10... | collective-permute-start | bytes 497672 | tf_op jit(solution)/shard_map/ppermute | solution.py:488
  26.1 11.7 %collective-permute-start.7 = (bf16[9,72,128]{2,1,0:T(8,128)(2,1)S(1)}, bf16[9,72,128]{2,1,0:T(8,128)(2,1)S(1)}, u32[]{:S(2)}, u32[]{:S(2)}) collective-permute-start(bf16[9,72,128]{2,1,0:T(8,128)(2,1)S(1)} %get-tuple-element.35), channel_id=1, source_target_pairs={{0,24},{8,16},{16,8},{24,0},{1,25},{9,17},{17,9},{25,1},{2,26},{10... | collective-permute-start | bytes 497672 | tf_op jit(solution)/shard_map/ppermute | solution.py:488
  28.2 18.3 %all-to-all-start = ((f32[32,1,128]{2,1,0:T(1,128)}), f32[32,1,128]{2,1,0:T(1,128)S(1)}, u32[]{:S(2)}, u32[]{:S(2)}) async-start(f32[32,1,128]{2,1,0:T(1,128)} %bitcast.3), calls=%async_computation | async-start | bytes 32768 | tf_op jit(solution)/shard_map/all_to_all | solution.py:482
  37.9 0.6 copy-start.4
  38.5 19.1 %collective-permute-start.9 = (bf16[8,288,128]{2,1,0:T(8,128)(2,1)S(1)}, bf16[8,288,128]{2,1,0:T(8,128)(2,1)S(1)}, u32[]{:S(2)}, u32[]{:S(2)}) collective-permute-start(bf16[8,288,128]{2,1,0:T(8,128)(2,1)S(1)} %get-tuple-element.36.refs_6_), channel_id=1, source_target_pairs={{0,1},{1,0},{2,3},{3,2},{4,5},{5,4},{6,7},{7,6},{8,9},{9,8},{10,11... | collective-permute-start | bytes 1769480 | tf_op jit(solution)/shard_map/ppermute | solution.py:504
  42.7 15.0 %collective-permute-start.8 = (bf16[8,288,128]{2,1,0:T(8,128)(2,1)S(1)}, bf16[8,288,128]{2,1,0:T(8,128)(2,1)S(1)}, u32[]{:S(2)}, u32[]{:S(2)}) collective-permute-start(bf16[8,288,128]{2,1,0:T(8,128)(2,1)S(1)} %get-tuple-element.36.refs_6_), channel_id=1, source_target_pairs={{1,2},{3,4},{5,6},{2,1},{4,3},{6,5},{9,10},{11,12},{13,14},{10,9},... | collective-permute-start | bytes 1769480 | tf_op jit(solution)/shard_map/ppermute | solution.py:503
  46.5 0.9 copy-start.3
  47.4 10.2 %copy-start.5 = (bf16[1,288,128]{2,1,0:T(8,128)(2,1)S(1)}, bf16[1,288,128]{2,1,0:T(8,128)(2,1)}, u32[]{:S(2)}) copy-start(bf16[1,288,128]{2,1,0:T(8,128)(2,1)} %copy-done.4) | copy-start | bytes 221188

commit v3 on v2

--- a/solution.py
+++ b/solution.py
@@ -12,8 +12,7 @@
 bf16 = jnp.bfloat16
 f32 = jnp.float32
 MIB = 2**20
-CUTS = (0.5,)
-TIED = 2
+CUTS = (0.5625,)
 
 vmem = pl.BlockSpec(memory_space=pltpu.VMEM)
 smem = pl.BlockSpec(memory_space=pltpu.SMEM)
@@ -432,11 +431,12 @@
     )(core, *operands)
 
 
-def finish_kernel(scales, moved_ref, conv_ref, diss_ref, total):
+def finish_kernel(scales, moved_ref, conv_ref, diss_ref, total, rows_ref):
     total[...] = jnp.sum(moved_ref[...].astype(f32), axis=0)
-    groups = conv_ref.shape[0] // 8
+    groups = conv_ref.shape[1] // 8
     for number, rows in enumerate(unpack(total, 0, groups)):
-        conv_ref[pl.ds(number, groups, stride=8), :] = rows * scales[0]
+        rows_ref[pl.ds(number, groups, stride=8), :] = rows * scales[0]
+    conv_ref[...] = rows_ref[...].T
     first = 3 * groups
     groups = diss_ref.shape[0] // 8
     for number, rows in enumerate(unpack(total, first, groups)):
@@ -444,20 +444,23 @@
 
 
 def finish(moved, mode_count, scales):
-    devices = moved.shape[0]
-    return pl.pallas_call(
+    share = mode_count * mode_count // moved.shape[0]
+    conv, diss = pl.pallas_call(
         functools.partial(finish_kernel, scales),
         in_specs=[vmem],
         out_specs=(vmem, vmem),
         out_shape=(
-            jax.ShapeDtypeStruct((mode_count * mode_count // devices, mode_count), f32),
+            jax.ShapeDtypeStruct((mode_count, share), f32),
             jax.ShapeDtypeStruct((mode_count, mode_count), f32),
         ),
-        scratch_shapes=[pltpu.VMEM(moved.shape[1:], f32)],
+        scratch_shapes=[
+            pltpu.VMEM(moved.shape[1:], f32),
+            pltpu.VMEM((share, mode_count), f32),
+        ],
         compiler_params=room(moved, jax.ShapeDtypeStruct(moved.shape, f32)),
-        cost_estimate=cost(0.8),
         name="finish",
     )(moved)
+    return conv.T, diss
 
 
 def per_device(modes, volume):
@@ -479,7 +482,6 @@
     messages = head(me, modes, owners, spans)
 
     weights = pack(volume, messages[0][0], owners, planes)
-    weights = lax.all_to_all(weights, ("mode", "slab"), 0, 0, tiled=True)
 
     def exchange(blocks):
         moved = [blocks[0]]
@@ -495,17 +497,8 @@
     inter += [(j, i) for i, j in inter]
     intra = [(i, i ^ 1) for i in range(slabs)]
 
-    sources = []
-    for q in range(chunks):
-        edge = 0 if q == 0 else (spans[q][1] - spans[q][0] - 1 if q == chunks - 1 else None)
-        blocks = exchange(messages[q])
-        body, edge_row = assemble(me, blocks, edge)
-        between = lax.ppermute(body, "slab", inter)
-        within = lax.ppermute(body, "slab", intra)
-        sources += [body, edge_row, between, within]
-        if q + 1 < chunks:
-            tied = TIED
-            *held, messages[q + 1] = lax.optimization_barrier((*blocks[1 : 1 + tied], messages[q + 1]))
+    def after(value, *others):
+        return lax.optimization_barrier((value, *others))[0]
 
     def place(row):
         if row < 0:
@@ -515,23 +508,41 @@
         q = max(q for q in range(chunks) if cuts[q] <= row)
         return (4 * q, row - cuts[q])
 
-    sums = None
     share = mode_count**3 // devices
     fast = share % 384 == 0 and mode_count == 48
     message = (devices, (share + mode_count**2) // 128, 128) if fast else None
-    for q in range(chunks):
-        last = q == chunks - 1
-        start = cuts[q] - (q > 0)
-        stop = pairs if last else cuts[q + 1] - 1
+
+    def contraction(start, stop, sums, weights):
+        last = stop == pairs
         field_plan = [place(row) for row in range(start - 1, stop + 1)]
         halo_plan = []
         for row in range(start, stop):
             operand, inner = place(row)
             halo_plan.append((operand + 2, operand + 3, inner, row))
-        sums = galerkin(
+        return galerkin(
             position, sums, weights, sources, field_plan, halo_plan, rows_y,
             cells // owners, message if last else None,
         )
+
+    sources = []
+    blocks = exchange(messages[0])
+    for q in range(chunks):
+        edge = 0 if q == 0 else (spans[q][1] - spans[q][0] - 1 if q == chunks - 1 else None)
+        body, edge_row = assemble(me, blocks, edge)
+        between = lax.ppermute(body, "slab", inter)
+        within = lax.ppermute(body, "slab", intra)
+        sources += [body, edge_row, between, within]
+        if q == 0:
+            weights = lax.all_to_all(after(weights, body), ("mode", "slab"), 0, 0, tiled=True)
+        if q + 1 < chunks:
+            blocks = exchange([after(message, *blocks[1:3]) for message in messages[q + 1]])
+
+    sums = None
+    done = 0
+    for q in range(chunks):
+        stop = pairs if q == chunks - 1 else cuts[q + 1] - 1
+        sums = contraction(done, stop, sums, weights)
+        done = stop
 
     total_cells = cells * rows_y * planes * slabs
     scales = (1.0 / math.sqrt(total_cells), viscosity / total_cells)

time: 94.5 us -> 91 us (0.963)
  blocking collectives: 22.1 us -> 19.6 us
    all_to_all x1, blocking collectives: 22.1 us -> 19.6 us  [per_device(): moved = lax.all_to_all(sums, ('mode', 'slab'), 0, 0, tiled=True)]
  transfers between devices with their start and end apart: 11 -> 11, of which waited for: 4 -> 4; matrix products, arithmetic and copies ran while one was open for 0% -> 0% of each run, Pallas kernels for 12% -> 13%
where the time goes in v3:
time: 91 us; the launch traced here: 90.7 us
  Pallas kernels  25.8 us (28%)
  starting transfers between devices  23.2 us (25%)
  blocking collectives  19.6 us (22%)
  waiting for transfers between devices  18.6 us (20%)
  local copies, waits for them, and re-layouts  2.77 us (3%)
    pallas_call x2, Pallas kernels, galerkin(): pl.pallas_call(functools.partial(galerkin_kernel, field_plan, halo_plan,...  22.8 us
    all_to_all x1, blocking collectives, per_device(): moved = lax.all_to_all(sums, ('mode', 'slab'), 0, 0, tiled=True)  19.6 us
    ppermute x6, waiting for transfers between devices, exchange(): lax.ppermute(blocks[shift], 'mode', [(source, source ^ shift) for source...  15.6 us
    ppermute x6, starting transfers between devices, exchange(): lax.ppermute(blocks[shift], 'mode', [(source, source ^ shift) for source...  11.3 us
    all_to_all x1, starting transfers between devices, per_device(): lax.all_to_all(after(weights, body), ('mode', 'slab'), 0, 0, tiled=True)  6.52 us
    ppermute x2, starting transfers between devices, per_device(): within = lax.ppermute(body, 'slab', intra)  4.01 us
    all_to_all x1, waiting for transfers between devices, per_device(): lax.all_to_all(after(weights, body), ('mode', 'slab'), 0, 0, tiled=True)  2.95 us
    unnamed x12, local copies, waits for them, and re-layouts  2.77 us
  transfers between devices with their start and end apart: 11, of which 4 were waited for; matrix products, arithmetic and copies ran while one was open for 0% of the time, Pallas kernels for 13%

profile of v3, /device:TPU:0, one launch (start us, length us, event | category | flops | bytes accessed | tf_op | source)
XLA Modules:
  0.0 90.7 jit_solution(18215446723193713278)
XLA Ops:
  0.6 0.0 copy-start
  0.6 1.3 %copy-done = bf16[12,3,2,64,128]{4,3,2,1,0:T(8,128)(2,1)S(1)} copy-done((bf16[12,3,2,64,128]{4,3,2,1,0:T(8,128)(2,1)S(1)}, bf16[12,3,2,64,128]{4,3,2,1,0:T(8,128)(2,1)}, u32[]{:S(2)}) %copy-start) | copy-done | bytes 1179672
  1.9 0.0 copy-start.1
  1.9 1.1 %head.1 = (bf16[10,72,128]{2,1,0:T(8,128)(2,1)S(1)}, bf16[10,72,128]{2,1,0:T(8,128)(2,1)S(1)}, bf16[10,72,128]{2,1,0:T(8,128)(2,1)S(1)}, bf16[10,72,128]{2,1,0:T...) custom-call(s32[1]{0:T(128)} %bitcast.1.me_ref, ...), custom_call_target="tpu_custom_call" | custom-call | flops 1000000000 | bytes 3000000 | tf_op jit(solution)/shard_map/head/pallas_call | solution.py:86
  3.0 3.1 %collective-permute-start = (bf16[10,72,128]{2,1,0:T(8,128)(2,1)S(1)}, bf16[10,72,128]{2,1,0:T(8,128)(2,1)S(1)}, u32[]{:S(2)}, u32[]{:S(2)}) collective-permute-start(bf16[10,72,128]{2,1,0:T(8,128)(2,1)S(1)} %get-tuple-element.24), channel_id=1, source_target_pairs={{0,8},{8,0},{16,24},{24,16},{1,9},{9,1},{17,25},{25,17},{2,10},{10... | collective-permute-start | bytes 552968 | tf_op jit(solution)/shard_map/ppermute | solution.py:490
  6.1 2.6 %collective-permute-start.1 = (bf16[10,72,128]{2,1,0:T(8,128)(2,1)S(1)}, bf16[10,72,128]{2,1,0:T(8,128)(2,1)S(1)}, u32[]{:S(2)}, u32[]{:S(2)}) collective-permute-start(bf16[10,72,128]{2,1,0:T(8,128)(2,1)S(1)} %get-tuple-element.25), channel_id=1, source_target_pairs={{0,16},{8,24},{16,0},{24,8},{1,17},{9,25},{17,1},{25,9},{2,18},{10... | collective-permute-start | bytes 552968 | tf_op jit(solution)/shard_map/ppermute | solution.py:490
  8.7 0.0 collective-permute-start.2
  8.7 5.1 %collective-permute-done.refs_1_ = bf16[10,72,128]{2,1,0:T(8,128)(2,1)S(1)} collective-permute-done((bf16[10,72,128]{2,1,0:T(8,128)(2,1)S(1)}, bf16[10,72,128]{2,1,0:T(8,128)(2,1)S(1)}, u32[]{:S(2)}, u32[]{:S(2)}) %collective-permute-start) | collective-permute-done | bytes 184352 | tf_op jit(solution)/shard_map/ppermute | solution.py:490
  13.8 8.7 %collective-permute-done.1.refs_2_ = bf16[10,72,128]{2,1,0:T(8,128)(2,1)S(1)} collective-permute-done((bf16[10,72,128]{2,1,0:T(8,128)(2,1)S(1)}, bf16[10,72,128]{2,1,0:T(8,128)(2,1)S(1)}, u32[]{:S(2)}, u32[]{:S(2)}) %collective-permute-start.1) | collective-permute-done | bytes 184352 | tf_op jit(solution)/shard_map/ppermute | solution.py:490
  22.4 0.0 collective-permute-done.2.refs_3_
  22.4 0.2 assemble.2
  22.6 0.0 copy-start.2
  22.6 0.1 collective-permute-start.4
  22.7 0.7 collective-permute-start.3
  23.4 3.2 %collective-permute-start.5 = (bf16[8,72,128]{2,1,0:T(8,128)(2,1)S(1)}, bf16[8,72,128]{2,1,0:T(8,128)(2,1)S(1)}, u32[]{:S(2)}, u32[]{:S(2)}) collective-permute-start(bf16[8,72,128]{2,1,0:T(8,128)(2,1)S(1)} %get-tuple-element.35), channel_id=1, source_target_pairs={{0,8},{8,0},{16,24},{24,16},{1,9},{9,1},{17,25},{25,17},{2,10},{10... | collective-permute-start | bytes 442376 | tf_op jit(solution)/shard_map/ppermute | solution.py:490
  26.6 1.1 %collective-permute-start.6 = (bf16[8,72,128]{2,1,0:T(8,128)(2,1)S(1)}, bf16[8,72,128]{2,1,0:T(8,128)(2,1)S(1)}, u32[]{:S(2)}, u32[]{:S(2)}) collective-permute-start(bf16[8,72,128]{2,1,0:T(8,128)(2,1)S(1)} %get-tuple-element.37), channel_id=1, source_target_pairs={{0,16},{8,24},{16,0},{24,8},{1,17},{9,25},{17,1},{25,9},{2,18},{10... | collective-permute-start | bytes 442376 | tf_op jit(solution)/shard_map/ppermute | solution.py:490
  27.7 1.4 %collective-permute-start.7 = (bf16[8,72,128]{2,1,0:T(8,128)(2,1)S(1)}, bf16[8,72,128]{2,1,0:T(8,128)(2,1)S(1)}, u32[]{:S(2)}, u32[]{:S(2)}) collective-permute-start(bf16[8,72,128]{2,1,0:T(8,128)(2,1)S(1)} %get-tuple-element.39), channel_id=1, source_target_pairs={{0,24},{8,16},{16,8},{24,0},{1,25},{9,17},{17,9},{25,1},{2,26},{10... | collective-permute-start | bytes 442376 | tf_op jit(solution)/shard_map/ppermute | solution.py:490
  29.1 0.0 copy-done.1
  29.1 0.7 pack.1
  29.8 0.0 copy-done.2
  29.8 6.5 %all-to-all-start = ((f32[32,1,128]{2,1,0:T(1,128)}), f32[32,1,128]{2,1,0:T(1,128)S(1)}, u32[]{:S(2)}, u32[]{:S(2)}) async-start(f32[32,1,128]{2,1,0:T(1,128)} %bitcast.3), calls=%async_computation | async-start | bytes 32768 | tf_op jit(solution)/shard_map/all_to_all | solution.py:536
  36.3 0.0 collective-permute-done.5.refs_1_
  36.3 0.0 collective-permute-done.6.refs_2_
  36.3 1.9 %collective-permute-done.7.refs_3_ = bf16[8,72,128]{2,1,0:T(8,128)(2,1)S(1)} collective-permute-done((bf16[8,72,128]{2,1,0:T(8,128)(2,1)S(1)}, bf16[8,72,128]{2,1,0:T(8,128)(2,1)S(1)}, u32[]{:S(2)}, u32[]{:S(2)}) %collective-permute-start.7) | collective-permute-done | bytes 147488 | tf_op jit(solution)/shard_map/ppermute | solution.py:490
  38.2 0.1 assemble.3
  38.3 0.0 copy-start.4
  38.3 0.6 copy-done.4
  38.9 3.9 %collective-permute-start.9 = (bf16[7,288,128]{2,1,0:T(8,128)(2,1)S(1)}, bf16[7,288,128]{2,1,0:T(8,128)(2,1)S(1)}, u32[]{:S(2)}, u32[]{:S(2)}) collective-permute-start(bf16[7,288,128]{2,1,0:T(8,128)(2,1)S(1)} %get-tuple-element.40.refs_6_), channel_id=1, source_target_pairs={{0,1},{1,0},{2,3},{3,2},{4,5},{5,4},{6,7},{7,6},{8,9},{9,8},{10,11... | collective-permute-start | bytes 1548296 | tf_op jit(solution)/shard_map/ppermute | solution.py:533
  42.9 0.7 collective-permute-start.8
  43.6 3.0 %all-to-all-done = f32[32,1,128]{2,1,0:T(1,128)S(1)} async-done(((f32[32,1,128]{2,1,0:T(1,128)}), f32[32,1,128]{2,1,0:T(1,128)S(1)}, u32[]{:S(2)}, u32[]{:S(2)}) %all-to-all-start) | async-done | bytes 16416 | tf_op jit(solution)/shard_map/all_to_all | solution.py:536
  46.5 0.0 collective-permute-done.4.refs_4_.refs_5_
  46.5 0.0 collective-permute-done.3.refs_3_.refs_4_
  46.5 0.0 copy-start.3
  46.5 0.9 copy-done.3
  47.4 0.0 copy-start.5
  47.4 11.1 %galerkin.2 = (f32[2304,128]{1,0:T(8,128)S(1)}, f32[48,128]{1,0:T(8,128)S(1)}) custom-call(s32[1]{0:T(128)} %bitcast.core_ref, f32[32,128]{1,0:T(8,128)S(1)} %bitcast.7, bf16[9,288,128]{2,1,0:T(8,128)(2,1)S(1)} %get-tuple-element.27.refs_1_.refs_3_, bf16[1,288,128]{2,1,0:T(8,128)(2,1)S(1)} %copy-done.3, ...), custom_call_target="tpu_custom_call" | custom-call | flops 11699999744 | bytes 35100000 | tf_op jit(solution)/shard_map/galerkin/pallas_call | solution.py:419
  58.5 0.0 collective-permute-done.9.refs_9_
  58.6 0.0 collective-permute-done.8.refs_8_
  58.6 0.0 copy-done.5
  58.6 11.7 %galerkin.3 = bf16[32,45,128]{2,1,0:T(8,128)(2,1)S(1)} custom-call(s32[1]{0:T(128)} %bitcast.core_ref, f32[2304,128]{1,0:T(8,128)S(1)} %get-tuple-element.30.refs_0_, f32[48,128]{1,0:T(8,128)S(1)} %get-tuple-element.31.refs_1_, f32[32,128]{1,0:T(8,128)S(1)} %bitcast.8, bf16[9,288,128]{2,1,0:T(8,128)(2,1)S(1)} %get-tuple-element.27.refs_1_.refs_3_, ...), custom_call_target="tpu_custom_call" | custom-call | flops 11699999744 | bytes 35100000 | tf_op jit(solution)/shard_map/galerkin/pallas_call | solution.py:419
  70.3 19.6 %all_to_all.16.moved_ref = bf16[32,45,128]{2,1,0:T(8,128)(2,1)S(1)} all-to-all(bf16[32,45,128]{2,1,0:T(8,128)(2,1)S(1)} %galerkin.3), channel_id=1, replica_groups=mesh['mode'=4,'slab'=8] {'mode','slab'}, dimensions={0} | all-to-all | bytes 737280 | tf_op jit(solution)/shard_map/all_to_all | solution.py:550
  89.9 0.8 finish.1
Async XLA Ops:
  0.6 1.3 %copy-start = (bf16[12,3,2,64,128]{4,3,2,1,0:T(8,128)(2,1)S(1)}, bf16[12,3,2,64,128]{4,3,2,1,0:T(8,128)(2,1)}, u32[]{:S(2)}) copy-start(bf16[12,3,2,64,128]{4,3,2,1,0:T(8,128)(2,1)} %modes_ref.1) | copy-start | bytes 3538948
  1.9 27.2 %copy-start.1 = (f32[16,2,128]{2,1,0:T(2,128)S(1)}, f32[16,2,128]{2,1,0:T(2,128)}, u32[]{:S(2)}) copy-start(f32[16,2,128]{2,1,0:T(2,128)} %volume_ref.1) | copy-start | bytes 49156
  3.0 10.8 %collective-permute-start = (bf16[10,72,128]{2,1,0:T(8,128)(2,1)S(1)}, bf16[10,72,128]{2,1,0:T(8,128)(2,1)S(1)}, u32[]{:S(2)}, u32[]{:S(2)}) collective-permute-start(bf16[10,72,128]{2,1,0:T(8,128)(2,1)S(1)} %get-tuple-element.24), channel_id=1, source_target_pairs={{0,8},{8,0},{16,24},{24,16},{1,9},{9,1},{17,25},{25,17},{2,10},{10... | collective-permute-start | bytes 552968 | tf_op jit(solution)/shard_map/ppermute | solution.py:490
  6.1 16.4 %collective-permute-start.1 = (bf16[10,72,128]{2,1,0:T(8,128)(2,1)S(1)}, bf16[10,72,128]{2,1,0:T(8,128)(2,1)S(1)}, u32[]{:S(2)}, u32[]{:S(2)}) collective-permute-start(bf16[10,72,128]{2,1,0:T(8,128)(2,1)S(1)} %get-tuple-element.25), channel_id=1, source_target_pairs={{0,16},{8,24},{16,0},{24,8},{1,17},{9,25},{17,1},{25,9},{2,18},{10... | collective-permute-start | bytes 552968 | tf_op jit(solution)/shard_map/ppermute | solution.py:490
  8.7 13.8 %collective-permute-start.2 = (bf16[10,72,128]{2,1,0:T(8,128)(2,1)S(1)}, bf16[10,72,128]{2,1,0:T(8,128)(2,1)S(1)}, u32[]{:S(2)}, u32[]{:S(2)}) collective-permute-start(bf16[10,72,128]{2,1,0:T(8,128)(2,1)S(1)} %get-tuple-element.26), channel_id=1, source_target_pairs={{0,24},{8,16},{16,8},{24,0},{1,25},{9,17},{17,9},{25,1},{2,26},{10... | collective-permute-start | bytes 552968 | tf_op jit(solution)/shard_map/ppermute | solution.py:490
  22.6 7.1 %copy-start.2 = (bf16[1,288,128]{2,1,0:T(8,128)(2,1)}, bf16[1,288,128]{2,1,0:T(8,128)(2,1)S(1)}, u32[]{:S(2)}) copy-start(bf16[1,288,128]{2,1,0:T(8,128)(2,1)S(1)} %get-tuple-element.29.refs_2_) | copy-start | bytes 221188
  22.6 23.9 %collective-permute-start.4 = (bf16[9,288,128]{2,1,0:T(8,128)(2,1)S(1)}, bf16[9,288,128]{2,1,0:T(8,128)(2,1)S(1)}, u32[]{:S(2)}, u32[]{:S(2)}) collective-permute-start(bf16[9,288,128]{2,1,0:T(8,128)(2,1)S(1)} %get-tuple-element.27.refs_1_.refs_3_), channel_id=1, source_target_pairs={{0,1},{1,0},{2,3},{3,2},{4,5},{5,4},{6,7},{7,6},{8,9},{9,8},{10,11... | collective-permute-start | bytes 1990664 | tf_op jit(solution)/shard_map/ppermute | solution.py:533
  22.7 23.8 %collective-permute-start.3 = (bf16[9,288,128]{2,1,0:T(8,128)(2,1)S(1)}, bf16[9,288,128]{2,1,0:T(8,128)(2,1)S(1)}, u32[]{:S(2)}, u32[]{:S(2)}) collective-permute-start(bf16[9,288,128]{2,1,0:T(8,128)(2,1)S(1)} %get-tuple-element.27.refs_1_.refs_3_), channel_id=1, source_target_pairs={{1,2},{3,4},{5,6},{2,1},{4,3},{6,5},{9,10},{11,12},{13,14},{10,9},... | collective-permute-start | bytes 1990664 | tf_op jit(solution)/shard_map/ppermute | solution.py:532
  23.4 12.9 %collective-permute-start.5 = (bf16[8,72,128]{2,1,0:T(8,128)(2,1)S(1)}, bf16[8,72,128]{2,1,0:T(8,128)(2,1)S(1)}, u32[]{:S(2)}, u32[]{:S(2)}) collective-permute-start(bf16[8,72,128]{2,1,0:T(8,128)(2,1)S(1)} %get-tuple-element.35), channel_id=1, source_target_pairs={{0,8},{8,0},{16,24},{24,16},{1,9},{9,1},{17,25},{25,17},{2,10},{10... | collective-permute-start | bytes 442376 | tf_op jit(solution)/shard_map/ppermute | solution.py:490
  26.6 9.7 %collective-permute-start.6 = (bf16[8,72,128]{2,1,0:T(8,128)(2,1)S(1)}, bf16[8,72,128]{2,1,0:T(8,128)(2,1)S(1)}, u32[]{:S(2)}, u32[]{:S(2)}) collective-permute-start(bf16[8,72,128]{2,1,0:T(8,128)(2,1)S(1)} %get-tuple-element.37), channel_id=1, source_target_pairs={{0,16},{8,24},{16,0},{24,8},{1,17},{9,25},{17,1},{25,9},{2,18},{10... | collective-permute-start | bytes 442376 | tf_op jit(solution)/shard_map/ppermute | solution.py:490
  27.7 10.5 %collective-permute-start.7 = (bf16[8,72,128]{2,1,0:T(8,128)(2,1)S(1)}, bf16[8,72,128]{2,1,0:T(8,128)(2,1)S(1)}, u32[]{:S(2)}, u32[]{:S(2)}) collective-permute-start(bf16[8,72,128]{2,1,0:T(8,128)(2,1)S(1)} %get-tuple-element.39), channel_id=1, source_target_pairs={{0,24},{8,16},{16,8},{24,0},{1,25},{9,17},{17,9},{25,1},{2,26},{10... | collective-permute-start | bytes 442376 | tf_op jit(solution)/shard_map/ppermute | solution.py:490
  29.8 16.8 %all-to-all-start = ((f32[32,1,128]{2,1,0:T(1,128)}), f32[32,1,128]{2,1,0:T(1,128)S(1)}, u32[]{:S(2)}, u32[]{:S(2)}) async-start(f32[32,1,128]{2,1,0:T(1,128)} %bitcast.3), calls=%async_computation | async-start | bytes 32768 | tf_op jit(solution)/shard_map/all_to_all | solution.py:536
  38.3 0.6 copy-start.4
  38.9 19.6 %collective-permute-start.9 = (bf16[7,288,128]{2,1,0:T(8,128)(2,1)S(1)}, bf16[7,288,128]{2,1,0:T(8,128)(2,1)S(1)}, u32[]{:S(2)}, u32[]{:S(2)}) collective-permute-start(bf16[7,288,128]{2,1,0:T(8,128)(2,1)S(1)} %get-tuple-element.40.refs_6_), channel_id=1, source_target_pairs={{0,1},{1,0},{2,3},{3,2},{4,5},{5,4},{6,7},{7,6},{8,9},{9,8},{10,11... | collective-permute-start | bytes 1548296 | tf_op jit(solution)/shard_map/ppermute | solution.py:533
  42.9 15.7 %collective-permute-start.8 = (bf16[7,288,128]{2,1,0:T(8,128)(2,1)S(1)}, bf16[7,288,128]{2,1,0:T(8,128)(2,1)S(1)}, u32[]{:S(2)}, u32[]{:S(2)}) collective-permute-start(bf16[7,288,128]{2,1,0:T(8,128)(2,1)S(1)} %get-tuple-element.40.refs_6_), channel_id=1, source_target_pairs={{1,2},{3,4},{5,6},{2,1},{4,3},{6,5},{9,10},{11,12},{13,14},{10,9},... | collective-permute-start | bytes 1548296 | tf_op jit(solution)/shard_map/ppermute | solution.py:532
  46.5 0.9 copy-start.3
  47.4 11.1 %copy-start.5 = (bf16[1,288,128]{2,1,0:T(8,128)(2,1)S(1)}, bf16[1,288,128]{2,1,0:T(8,128)(2,1)}, u32[]{:S(2)}) copy-start(bf16[1,288,128]{2,1,0:T(8,128)(2,1)} %copy-done.4) | copy-start | bytes 221188

commit v4 on v3

--- a/solution.py
+++ b/solution.py
@@ -177,16 +177,39 @@
     return ((first - fifth) * (1.0 / 12.0) + (fourth - second) * (8.0 / 12.0)).astype(bf16)
 
 
-def repack(ref, out, groups):
-    rows = [ref[pl.ds(number, groups, stride=8), :][:, :48] for number in range(8)]
-    out[pl.ds(0, groups, stride=3), :] = jnp.concatenate(
-        [rows[0], rows[1], rows[2][:, :32]], axis=1
-    )
-    out[pl.ds(1, groups, stride=3), :] = jnp.concatenate(
-        [rows[2][:, 32:], rows[3], rows[4], rows[5][:, :16]], axis=1
-    )
-    out[pl.ds(2, groups, stride=3), :] = jnp.concatenate(
-        [rows[5][:, 16:], rows[6], rows[7]], axis=1
+def halves(size):
+    row = lax.broadcasted_iota(jnp.int32, (size, size), 0)
+    column = lax.broadcasted_iota(jnp.int32, (size, size), 1)
+    return row, column
+
+
+def fold(square):
+    half = square.shape[0] // 2
+    row, column = halves(half)
+    first, last = square[:half, :half], square[half:, half:]
+    mixed = jnp.where(column >= row, first, last)
+    diagonal = jnp.sum(jnp.where(column == row, last, 0.0), axis=1, keepdims=True)
+    blank = jnp.zeros((half, 63 - 2 * half), f32)
+    folded = jnp.concatenate([square[:half, half:], mixed, diagonal, blank], axis=1)
+    return jnp.concatenate([folded[: half // 2], folded[half // 2 :]], axis=1)
+
+
+def unfold(wide, size):
+    half = size // 2
+    row, column = halves(half)
+    folded = jnp.concatenate([wide[:, :64], wide[:, 64:]], axis=0)
+    cross = folded[:, :half]
+    mixed = folded[:, half:size]
+    turned = mixed.T
+    first = jnp.where(column >= row, mixed, turned)
+    last = jnp.where(column < row, mixed, turned)
+    last = jnp.where(column == row, folded[:, size : size + 1], last)
+    return jnp.concatenate(
+        [
+            jnp.concatenate([first, cross], axis=1),
+            jnp.concatenate([cross.T, last], axis=1),
+        ],
+        axis=0,
     )
 
 
@@ -214,9 +237,9 @@
     fields, low, high, weights_ref, carried0, carried1 = refs[-6:]
     buffers = (refs[-14:-10], refs[-10:-6])
     if packs:
-        flat, packed_diss, diss_ref, conv_ref = refs[-18:-14]
-        message_ref = refs[-19]
-        sources = refs[:-19]
+        flat, diss_ref, conv_ref = refs[-17:-14]
+        message_ref = refs[-18]
+        sources = refs[:-18]
     else:
         conv_ref, diss_ref = refs[-16:-14]
         sources = refs[:-16]
@@ -365,10 +388,9 @@
             flat[pl.ds(chunk, mode_count, stride=chunks), :] = (
                 part[:mode_count] + part[mode_count : 2 * mode_count]
             )
-        repack(diss_ref, packed_diss, mode_count // 8)
         devices, total, unused = message_ref.shape
-        share = total - packed_diss.shape[0]
-        tail = packed_diss[...]
+        tail = fold(diss_ref[:, :mode_count])
+        share = total - tail.shape[0]
         for device in range(devices):
             message_ref[device] = jnp.concatenate(
                 [flat[device * share : (device + 1) * share, :], tail], axis=0
@@ -394,7 +416,6 @@
         out_shape = jax.ShapeDtypeStruct(message, bf16)
         scratch = [
             pltpu.VMEM((mode_count * square // 128, 128), f32),
-            pltpu.VMEM((square // 128, 128), f32),
             pltpu.VMEM((mode_count, 128), f32),
             pltpu.VMEM((square, 128), f32),
         ]
@@ -437,10 +458,7 @@
     for number, rows in enumerate(unpack(total, 0, groups)):
         rows_ref[pl.ds(number, groups, stride=8), :] = rows * scales[0]
     conv_ref[...] = rows_ref[...].T
-    first = 3 * groups
-    groups = diss_ref.shape[0] // 8
-    for number, rows in enumerate(unpack(total, first, groups)):
-        diss_ref[pl.ds(number, groups, stride=8), :] = rows * scales[1]
+    diss_ref[...] = unfold(total[3 * groups :, :], diss_ref.shape[0]) * scales[1]
 
 
 def finish(moved, mode_count, scales):
@@ -510,7 +528,7 @@
 
     share = mode_count**3 // devices
     fast = share % 384 == 0 and mode_count == 48
-    message = (devices, (share + mode_count**2) // 128, 128) if fast else None
+    message = (devices, share // 128 + mode_count // 4, 128) if fast else None
 
     def contraction(start, stop, sums, weights):
         last = stop == pairs

time: 91 us -> 90.2 us (level)
  blocking collectives: 19.6 us -> 18.1 us
    all_to_all x1, blocking collectives: 19.6 us -> 18.1 us  [per_device(): moved = lax.all_to_all(sums, ('mode', 'slab'), 0, 0, tiled=True)]
  transfers between devices with their start and end apart: 11 -> 11, of which waited for: 4 -> 4; matrix products, arithmetic and copies ran while one was open for 0% -> 0% of each run, Pallas kernels for 13% -> 14%
where the time goes in v4:
time: 90.2 us; the launch traced here: 89.9 us
  Pallas kernels  26.5 us (29%)
  starting transfers between devices  23.2 us (26%)
  waiting for transfers between devices  18.6 us (21%)
  blocking collectives  18.1 us (20%)
  local copies, waits for them, and re-layouts  2.77 us (3%)
    pallas_call x2, Pallas kernels, galerkin(): pl.pallas_call(functools.partial(galerkin_kernel, field_plan, halo_plan,...  23.4 us
    all_to_all x1, blocking collectives, per_device(): moved = lax.all_to_all(sums, ('mode', 'slab'), 0, 0, tiled=True)  18.1 us
    ppermute x6, waiting for transfers between devices, exchange(): lax.ppermute(blocks[shift], 'mode', [(source, source ^ shift) for source...  15.6 us
    ppermute x6, starting transfers between devices, exchange(): lax.ppermute(blocks[shift], 'mode', [(source, source ^ shift) for source...  11.3 us
    all_to_all x1, starting transfers between devices, per_device(): lax.all_to_all(after(weights, body), ('mode', 'slab'), 0, 0, tiled=True)  6.52 us
    ppermute x2, starting transfers between devices, per_device(): within = lax.ppermute(body, 'slab', intra)  4.01 us
    all_to_all x1, waiting for transfers between devices, per_device(): lax.all_to_all(after(weights, body), ('mode', 'slab'), 0, 0, tiled=True)  2.95 us
    unnamed x12, local copies, waits for them, and re-layouts  2.77 us
  transfers between devices with their start and end apart: 11, of which 4 were waited for; matrix products, arithmetic and copies ran while one was open for 0% of the time, Pallas kernels for 14%

profile of v4, /device:TPU:0, one launch (start us, length us, event | category | flops | bytes accessed | tf_op | source)
XLA Modules:
  0.0 89.9 jit_solution(12114358987130576759)
XLA Ops:
  0.6 0.0 copy-start
  0.6 1.3 %copy-done = bf16[12,3,2,64,128]{4,3,2,1,0:T(8,128)(2,1)S(1)} copy-done((bf16[12,3,2,64,128]{4,3,2,1,0:T(8,128)(2,1)S(1)}, bf16[12,3,2,64,128]{4,3,2,1,0:T(8,128)(2,1)}, u32[]{:S(2)}) %copy-start) | copy-done | bytes 1179672
  1.9 0.0 copy-start.1
  1.9 1.1 %head.1 = (bf16[10,72,128]{2,1,0:T(8,128)(2,1)S(1)}, bf16[10,72,128]{2,1,0:T(8,128)(2,1)S(1)}, bf16[10,72,128]{2,1,0:T(8,128)(2,1)S(1)}, bf16[10,72,128]{2,1,0:T...) custom-call(s32[1]{0:T(128)} %bitcast.1.me_ref, ...), custom_call_target="tpu_custom_call" | custom-call | flops 1000000000 | bytes 3000000 | tf_op jit(solution)/shard_map/head/pallas_call | solution.py:86
  3.0 3.1 %collective-permute-start = (bf16[10,72,128]{2,1,0:T(8,128)(2,1)S(1)}, bf16[10,72,128]{2,1,0:T(8,128)(2,1)S(1)}, u32[]{:S(2)}, u32[]{:S(2)}) collective-permute-start(bf16[10,72,128]{2,1,0:T(8,128)(2,1)S(1)} %get-tuple-element.24), channel_id=1, source_target_pairs={{0,8},{8,0},{16,24},{24,16},{1,9},{9,1},{17,25},{25,17},{2,10},{10... | collective-permute-start | bytes 552968 | tf_op jit(solution)/shard_map/ppermute | solution.py:508
  6.1 2.6 %collective-permute-start.1 = (bf16[10,72,128]{2,1,0:T(8,128)(2,1)S(1)}, bf16[10,72,128]{2,1,0:T(8,128)(2,1)S(1)}, u32[]{:S(2)}, u32[]{:S(2)}) collective-permute-start(bf16[10,72,128]{2,1,0:T(8,128)(2,1)S(1)} %get-tuple-element.25), channel_id=1, source_target_pairs={{0,16},{8,24},{16,0},{24,8},{1,17},{9,25},{17,1},{25,9},{2,18},{10... | collective-permute-start | bytes 552968 | tf_op jit(solution)/shard_map/ppermute | solution.py:508
  8.7 0.0 collective-permute-start.2
  8.7 5.1 %collective-permute-done.refs_1_ = bf16[10,72,128]{2,1,0:T(8,128)(2,1)S(1)} collective-permute-done((bf16[10,72,128]{2,1,0:T(8,128)(2,1)S(1)}, bf16[10,72,128]{2,1,0:T(8,128)(2,1)S(1)}, u32[]{:S(2)}, u32[]{:S(2)}) %collective-permute-start) | collective-permute-done | bytes 184352 | tf_op jit(solution)/shard_map/ppermute | solution.py:508
  13.8 8.7 %collective-permute-done.1.refs_2_ = bf16[10,72,128]{2,1,0:T(8,128)(2,1)S(1)} collective-permute-done((bf16[10,72,128]{2,1,0:T(8,128)(2,1)S(1)}, bf16[10,72,128]{2,1,0:T(8,128)(2,1)S(1)}, u32[]{:S(2)}, u32[]{:S(2)}) %collective-permute-start.1) | collective-permute-done | bytes 184352 | tf_op jit(solution)/shard_map/ppermute | solution.py:508
  22.4 0.0 collective-permute-done.2.refs_3_
  22.4 0.2 assemble.2
  22.6 0.0 copy-start.2
  22.6 0.1 collective-permute-start.4
  22.7 0.7 collective-permute-start.3
  23.4 3.2 %collective-permute-start.5 = (bf16[8,72,128]{2,1,0:T(8,128)(2,1)S(1)}, bf16[8,72,128]{2,1,0:T(8,128)(2,1)S(1)}, u32[]{:S(2)}, u32[]{:S(2)}) collective-permute-start(bf16[8,72,128]{2,1,0:T(8,128)(2,1)S(1)} %get-tuple-element.35), channel_id=1, source_target_pairs={{0,8},{8,0},{16,24},{24,16},{1,9},{9,1},{17,25},{25,17},{2,10},{10... | collective-permute-start | bytes 442376 | tf_op jit(solution)/shard_map/ppermute | solution.py:508
  26.6 1.1 %collective-permute-start.6 = (bf16[8,72,128]{2,1,0:T(8,128)(2,1)S(1)}, bf16[8,72,128]{2,1,0:T(8,128)(2,1)S(1)}, u32[]{:S(2)}, u32[]{:S(2)}) collective-permute-start(bf16[8,72,128]{2,1,0:T(8,128)(2,1)S(1)} %get-tuple-element.37), channel_id=1, source_target_pairs={{0,16},{8,24},{16,0},{24,8},{1,17},{9,25},{17,1},{25,9},{2,18},{10... | collective-permute-start | bytes 442376 | tf_op jit(solution)/shard_map/ppermute | solution.py:508
  27.7 1.4 %collective-permute-start.7 = (bf16[8,72,128]{2,1,0:T(8,128)(2,1)S(1)}, bf16[8,72,128]{2,1,0:T(8,128)(2,1)S(1)}, u32[]{:S(2)}, u32[]{:S(2)}) collective-permute-start(bf16[8,72,128]{2,1,0:T(8,128)(2,1)S(1)} %get-tuple-element.39), channel_id=1, source_target_pairs={{0,24},{8,16},{16,8},{24,0},{1,25},{9,17},{17,9},{25,1},{2,26},{10... | collective-permute-start | bytes 442376 | tf_op jit(solution)/shard_map/ppermute | solution.py:508
  29.1 0.0 copy-done.1
  29.1 0.7 pack.1
  29.8 0.0 copy-done.2
  29.8 6.5 %all-to-all-start = ((f32[32,1,128]{2,1,0:T(1,128)}), f32[32,1,128]{2,1,0:T(1,128)S(1)}, u32[]{:S(2)}, u32[]{:S(2)}) async-start(f32[32,1,128]{2,1,0:T(1,128)} %bitcast.3), calls=%async_computation | async-start | bytes 32768 | tf_op jit(solution)/shard_map/all_to_all | solution.py:554
  36.3 0.0 collective-permute-done.5.refs_1_
  36.3 0.0 collective-permute-done.6.refs_2_
  36.3 1.9 %collective-permute-done.7.refs_3_ = bf16[8,72,128]{2,1,0:T(8,128)(2,1)S(1)} collective-permute-done((bf16[8,72,128]{2,1,0:T(8,128)(2,1)S(1)}, bf16[8,72,128]{2,1,0:T(8,128)(2,1)S(1)}, u32[]{:S(2)}, u32[]{:S(2)}) %collective-permute-start.7) | collective-permute-done | bytes 147488 | tf_op jit(solution)/shard_map/ppermute | solution.py:508
  38.2 0.1 assemble.3
  38.3 0.0 copy-start.4
  38.3 0.6 copy-done.4
  38.9 3.9 %collective-permute-start.9 = (bf16[7,288,128]{2,1,0:T(8,128)(2,1)S(1)}, bf16[7,288,128]{2,1,0:T(8,128)(2,1)S(1)}, u32[]{:S(2)}, u32[]{:S(2)}) collective-permute-start(bf16[7,288,128]{2,1,0:T(8,128)(2,1)S(1)} %get-tuple-element.40.refs_6_), channel_id=1, source_target_pairs={{0,1},{1,0},{2,3},{3,2},{4,5},{5,4},{6,7},{7,6},{8,9},{9,8},{10,11... | collective-permute-start | bytes 1548296 | tf_op jit(solution)/shard_map/ppermute | solution.py:551
  42.9 0.7 collective-permute-start.8
  43.6 3.0 %all-to-all-done = f32[32,1,128]{2,1,0:T(1,128)S(1)} async-done(((f32[32,1,128]{2,1,0:T(1,128)}), f32[32,1,128]{2,1,0:T(1,128)S(1)}, u32[]{:S(2)}, u32[]{:S(2)}) %all-to-all-start) | async-done | bytes 16416 | tf_op jit(solution)/shard_map/all_to_all | solution.py:554
  46.5 0.0 collective-permute-done.4.refs_4_.refs_5_
  46.5 0.0 collective-permute-done.3.refs_3_.refs_4_
  46.5 0.0 copy-start.3
  46.5 0.9 copy-done.3
  47.4 0.0 copy-start.5
  47.4 11.4 %galerkin.2 = (f32[2304,128]{1,0:T(8,128)S(1)}, f32[48,128]{1,0:T(8,128)S(1)}) custom-call(s32[1]{0:T(128)} %bitcast.core_ref, f32[32,128]{1,0:T(8,128)S(1)} %bitcast.7, bf16[9,288,128]{2,1,0:T(8,128)(2,1)S(1)} %get-tuple-element.27.refs_1_.refs_3_, bf16[1,288,128]{2,1,0:T(8,128)(2,1)S(1)} %copy-done.3, ...), custom_call_target="tpu_custom_call" | custom-call | flops 11699999744 | bytes 35100000 | tf_op jit(solution)/shard_map/galerkin/pallas_call | solution.py:440
  58.9 0.0 collective-permute-done.9.refs_9_
  58.9 0.0 collective-permute-done.8.refs_8_
  58.9 0.0 copy-done.5
  58.9 12.0 %galerkin.3 = bf16[32,39,128]{2,1,0:T(8,128)(2,1)S(1)} custom-call(s32[1]{0:T(128)} %bitcast.core_ref, f32[2304,128]{1,0:T(8,128)S(1)} %get-tuple-element.30.refs_0_, f32[48,128]{1,0:T(8,128)S(1)} %get-tuple-element.31.refs_1_, f32[32,128]{1,0:T(8,128)S(1)} %bitcast.8, bf16[9,288,128]{2,1,0:T(8,128)(2,1)S(1)} %get-tuple-element.27.refs_1_.refs_3_, ...), custom_call_target="tpu_custom_call" | custom-call | flops 11699999744 | bytes 35100000 | tf_op jit(solution)/shard_map/galerkin/pallas_call | solution.py:440
  70.9 18.1 %all_to_all.16.moved_ref = bf16[32,39,128]{2,1,0:T(8,128)(2,1)S(1)} all-to-all(bf16[32,39,128]{2,1,0:T(8,128)(2,1)S(1)} %galerkin.3), channel_id=1, replica_groups=mesh['mode'=4,'slab'=8] {'mode','slab'}, dimensions={0} | all-to-all | bytes 638976 | tf_op jit(solution)/shard_map/all_to_all | solution.py:568
  89.0 1.0 %finish.1 = (f32[48,72]{1,0:T(8,128)}, f32[48,48]{1,0:T(8,128)}) custom-call(bf16[32,39,128]{2,1,0:T(8,128)(2,1)S(1)} %all_to_all.16.moved_ref), custom_call_target="tpu_custom_call" | custom-call | tf_op jit(solution)/shard_map/finish/pallas_call | solution.py:466
Async XLA Ops:
  0.6 1.3 %copy-start = (bf16[12,3,2,64,128]{4,3,2,1,0:T(8,128)(2,1)S(1)}, bf16[12,3,2,64,128]{4,3,2,1,0:T(8,128)(2,1)}, u32[]{:S(2)}) copy-start(bf16[12,3,2,64,128]{4,3,2,1,0:T(8,128)(2,1)} %modes_ref.1) | copy-start | bytes 3538948
  1.9 27.2 %copy-start.1 = (f32[16,2,128]{2,1,0:T(2,128)S(1)}, f32[16,2,128]{2,1,0:T(2,128)}, u32[]{:S(2)}) copy-start(f32[16,2,128]{2,1,0:T(2,128)} %volume_ref.1) | copy-start | bytes 49156
  3.0 10.8 %collective-permute-start = (bf16[10,72,128]{2,1,0:T(8,128)(2,1)S(1)}, bf16[10,72,128]{2,1,0:T(8,128)(2,1)S(1)}, u32[]{:S(2)}, u32[]{:S(2)}) collective-permute-start(bf16[10,72,128]{2,1,0:T(8,128)(2,1)S(1)} %get-tuple-element.24), channel_id=1, source_target_pairs={{0,8},{8,0},{16,24},{24,16},{1,9},{9,1},{17,25},{25,17},{2,10},{10... | collective-permute-start | bytes 552968 | tf_op jit(solution)/shard_map/ppermute | solution.py:508
  6.1 16.4 %collective-permute-start.1 = (bf16[10,72,128]{2,1,0:T(8,128)(2,1)S(1)}, bf16[10,72,128]{2,1,0:T(8,128)(2,1)S(1)}, u32[]{:S(2)}, u32[]{:S(2)}) collective-permute-start(bf16[10,72,128]{2,1,0:T(8,128)(2,1)S(1)} %get-tuple-element.25), channel_id=1, source_target_pairs={{0,16},{8,24},{16,0},{24,8},{1,17},{9,25},{17,1},{25,9},{2,18},{10... | collective-permute-start | bytes 552968 | tf_op jit(solution)/shard_map/ppermute | solution.py:508
  8.7 13.8 %collective-permute-start.2 = (bf16[10,72,128]{2,1,0:T(8,128)(2,1)S(1)}, bf16[10,72,128]{2,1,0:T(8,128)(2,1)S(1)}, u32[]{:S(2)}, u32[]{:S(2)}) collective-permute-start(bf16[10,72,128]{2,1,0:T(8,128)(2,1)S(1)} %get-tuple-element.26), channel_id=1, source_target_pairs={{0,24},{8,16},{16,8},{24,0},{1,25},{9,17},{17,9},{25,1},{2,26},{10... | collective-permute-start | bytes 552968 | tf_op jit(solution)/shard_map/ppermute | solution.py:508
  22.6 7.1 %copy-start.2 = (bf16[1,288,128]{2,1,0:T(8,128)(2,1)}, bf16[1,288,128]{2,1,0:T(8,128)(2,1)S(1)}, u32[]{:S(2)}) copy-start(bf16[1,288,128]{2,1,0:T(8,128)(2,1)S(1)} %get-tuple-element.29.refs_2_) | copy-start | bytes 221188
  22.6 23.9 %collective-permute-start.4 = (bf16[9,288,128]{2,1,0:T(8,128)(2,1)S(1)}, bf16[9,288,128]{2,1,0:T(8,128)(2,1)S(1)}, u32[]{:S(2)}, u32[]{:S(2)}) collective-permute-start(bf16[9,288,128]{2,1,0:T(8,128)(2,1)S(1)} %get-tuple-element.27.refs_1_.refs_3_), channel_id=1, source_target_pairs={{0,1},{1,0},{2,3},{3,2},{4,5},{5,4},{6,7},{7,6},{8,9},{9,8},{10,11... | collective-permute-start | bytes 1990664 | tf_op jit(solution)/shard_map/ppermute | solution.py:551
  22.7 23.8 %collective-permute-start.3 = (bf16[9,288,128]{2,1,0:T(8,128)(2,1)S(1)}, bf16[9,288,128]{2,1,0:T(8,128)(2,1)S(1)}, u32[]{:S(2)}, u32[]{:S(2)}) collective-permute-start(bf16[9,288,128]{2,1,0:T(8,128)(2,1)S(1)} %get-tuple-element.27.refs_1_.refs_3_), channel_id=1, source_target_pairs={{1,2},{3,4},{5,6},{2,1},{4,3},{6,5},{9,10},{11,12},{13,14},{10,9},... | collective-permute-start | bytes 1990664 | tf_op jit(solution)/shard_map/ppermute | solution.py:550
  23.4 12.9 %collective-permute-start.5 = (bf16[8,72,128]{2,1,0:T(8,128)(2,1)S(1)}, bf16[8,72,128]{2,1,0:T(8,128)(2,1)S(1)}, u32[]{:S(2)}, u32[]{:S(2)}) collective-permute-start(bf16[8,72,128]{2,1,0:T(8,128)(2,1)S(1)} %get-tuple-element.35), channel_id=1, source_target_pairs={{0,8},{8,0},{16,24},{24,16},{1,9},{9,1},{17,25},{25,17},{2,10},{10... | collective-permute-start | bytes 442376 | tf_op jit(solution)/shard_map/ppermute | solution.py:508
  26.6 9.7 %collective-permute-start.6 = (bf16[8,72,128]{2,1,0:T(8,128)(2,1)S(1)}, bf16[8,72,128]{2,1,0:T(8,128)(2,1)S(1)}, u32[]{:S(2)}, u32[]{:S(2)}) collective-permute-start(bf16[8,72,128]{2,1,0:T(8,128)(2,1)S(1)} %get-tuple-element.37), channel_id=1, source_target_pairs={{0,16},{8,24},{16,0},{24,8},{1,17},{9,25},{17,1},{25,9},{2,18},{10... | collective-permute-start | bytes 442376 | tf_op jit(solution)/shard_map/ppermute | solution.py:508
  27.7 10.5 %collective-permute-start.7 = (bf16[8,72,128]{2,1,0:T(8,128)(2,1)S(1)}, bf16[8,72,128]{2,1,0:T(8,128)(2,1)S(1)}, u32[]{:S(2)}, u32[]{:S(2)}) collective-permute-start(bf16[8,72,128]{2,1,0:T(8,128)(2,1)S(1)} %get-tuple-element.39), channel_id=1, source_target_pairs={{0,24},{8,16},{16,8},{24,0},{1,25},{9,17},{17,9},{25,1},{2,26},{10... | collective-permute-start | bytes 442376 | tf_op jit(solution)/shard_map/ppermute | solution.py:508
  29.8 16.8 %all-to-all-start = ((f32[32,1,128]{2,1,0:T(1,128)}), f32[32,1,128]{2,1,0:T(1,128)S(1)}, u32[]{:S(2)}, u32[]{:S(2)}) async-start(f32[32,1,128]{2,1,0:T(1,128)} %bitcast.3), calls=%async_computation | async-start | bytes 32768 | tf_op jit(solution)/shard_map/all_to_all | solution.py:554
  38.3 0.6 copy-start.4
  38.9 19.9 %collective-permute-start.9 = (bf16[7,288,128]{2,1,0:T(8,128)(2,1)S(1)}, bf16[7,288,128]{2,1,0:T(8,128)(2,1)S(1)}, u32[]{:S(2)}, u32[]{:S(2)}) collective-permute-start(bf16[7,288,128]{2,1,0:T(8,128)(2,1)S(1)} %get-tuple-element.40.refs_6_), channel_id=1, source_target_pairs={{0,1},{1,0},{2,3},{3,2},{4,5},{5,4},{6,7},{7,6},{8,9},{9,8},{10,11... | collective-permute-start | bytes 1548296 | tf_op jit(solution)/shard_map/ppermute | solution.py:551
  42.9 16.0 %collective-permute-start.8 = (bf16[7,288,128]{2,1,0:T(8,128)(2,1)S(1)}, bf16[7,288,128]{2,1,0:T(8,128)(2,1)S(1)}, u32[]{:S(2)}, u32[]{:S(2)}) collective-permute-start(bf16[7,288,128]{2,1,0:T(8,128)(2,1)S(1)} %get-tuple-element.40.refs_6_), channel_id=1, source_target_pairs={{1,2},{3,4},{5,6},{2,1},{4,3},{6,5},{9,10},{11,12},{13,14},{10,9},... | collective-permute-start | bytes 1548296 | tf_op jit(solution)/shard_map/ppermute | solution.py:550
  46.5 0.9 copy-start.3
  47.4 11.5 %copy-start.5 = (bf16[1,288,128]{2,1,0:T(8,128)(2,1)S(1)}, bf16[1,288,128]{2,1,0:T(8,128)(2,1)}, u32[]{:S(2)}) copy-start(bf16[1,288,128]{2,1,0:T(8,128)(2,1)} %copy-done.4) | copy-start | bytes 221188
